TPU v7x, 128 devices: a whole 4x4x4 slice. The times are simulated.
128 devices in a mesh: feat: 8 (over y, core), node: 16 (over x, z).
Axes of the slice: x: 4, y: 4, z: 4, core: 2. Of those that a mesh axis runs over, the one named last changes fastest.
Arguments:
- features: bfloat16 [128, 98304], P('feat', 'node'), may hold values from -6 to 6
- tile_cols: int32 [768, 16], P('node'), may hold values from 0 to 767, as said below
- tile_counts: int32 [768], P('node'), may hold values from 1 to 16, as said below
- tiles: bfloat16 [768, 16, 128, 128], P('node'), may hold values from 0 to 2, as said below
- degrees: int32 [98304], P('node'), may hold values from 8 to 32
- weights1: bfloat16 [2, 128, 256], P(None, 'feat'), may hold values from -0.5 to 0.5
- bias1: float32 [256], replicated, may hold values from -3 to 3
- weights2: bfloat16 [2, 256, 256], P(None, 'feat'), may hold values from -0.375 to 0.375
- bias2: float32 [256], replicated, may hold values from -3 to 3
- cotangent: bfloat16 [98304, 256], P(('node', 'feat')), may hold values from -6 to 6
Outputs:
- hidden_out: bfloat16 [98304, 256], P(('node', 'feat'))
- grad_second: float32 [2, 256, 256], P(None, 'feat')
- grad_first: float32 [2, 128, 256], P(None, 'feat')
Inputs may be any that keep to these rules, and one draw needn't show every extreme that they name: `tile_cols`: the first tile_counts[r] column blocks of a row block are distinct; later slots are unused. `tile_counts`: 16 is reached in every draw; node shards differ in their load. `tiles`: each entry is zero or a positive edge weight.
All inputs are finite; a program needn't handle non-finite values.
Results may differ from a plain program's by a relative error of at most 0.0055.
Values may be sent and summed in bfloat16 or wider, within the bound.
A program may use at most 128 MiB of HBM per device.

v0:
```python
import math

import jax
import jax.numpy as jnp
from jax import lax
from jax.sharding import PartitionSpec as P


def aggregate(source, tile_cols, tile_counts, tiles):
    source_width = source.shape[0]
    tile_edge = tiles.shape[-1]
    blocks = source.reshape(source_width, source.shape[1] // tile_edge, tile_edge)
    picked = jnp.take(blocks, tile_cols, axis=1)
    alive_mask = (
        lax.broadcasted_iota(jnp.int32, tile_cols.shape, 1) < tile_counts[:, None]
    ).astype(source.dtype)
    picked = picked * alive_mask[None, :, :, None]
    summed = jnp.einsum("wbts,btds->wbd", picked, tiles, preferred_element_type=jnp.float32)
    return summed.reshape(source_width, -1)


def shards(
    features, tile_cols, tile_counts, tiles, degrees, weights1, bias1, weights2, bias2, cotangent
):
    feat_part = features.shape[0]
    hid_part = weights2.shape[1]
    hidden_width = weights2.shape[2]
    shard_nodes = features.shape[1]
    tile_edge = tiles.shape[-1]
    local_blocks = tiles.shape[0]
    slot_total = tiles.shape[1]
    degree_row = degrees.astype(jnp.float32)[None, :]
    all_feats = lax.all_gather(features, "node", axis=1, tiled=True)
    feat_mean = (aggregate(all_feats, tile_cols, tile_counts, tiles) / degree_row).astype(
        jnp.bfloat16
    )
    first_stack = jnp.concatenate([features, feat_mean], axis=0)
    first_weights = weights1.reshape(2 * feat_part, hidden_width)
    picked_cols = first_stack
    pre_first = (
        lax.psum_scatter(
            lax.dot_general(
                picked_cols,
                first_weights,
                (((0,), (0,)), ((), ())),
                preferred_element_type=jnp.float32,
            ),
            "feat",
            scatter_dimension=0,
            tiled=True,
        )
        + bias1
    )
    sigmoid_pre = jax.nn.sigmoid(pre_first)
    hidden = (pre_first * sigmoid_pre).astype(jnp.bfloat16)
    slope = (sigmoid_pre * (1.0 + pre_first * (1.0 - sigmoid_pre))).astype(jnp.bfloat16)
    hidden_cols, slope_cols = (
        lax.all_to_all(hidden.T, "feat", split_axis=0, concat_axis=1, tiled=True),
        lax.all_to_all(slope.T, "feat", split_axis=0, concat_axis=1, tiled=True),
    )
    all_hidden = lax.all_gather(hidden_cols, "node", axis=1, tiled=True)
    hidden_mean = (aggregate(all_hidden, tile_cols, tile_counts, tiles) / degree_row).astype(
        jnp.bfloat16
    )
    second_stack = jnp.concatenate([hidden_cols, hidden_mean], axis=0)
    second_weights = weights2.reshape(2 * hid_part, hidden_width)
    picked_cols = second_stack
    hidden_out = (
        lax.psum_scatter(
            lax.dot_general(
                picked_cols,
                second_weights,
                (((0,), (0,)), ((), ())),
                preferred_element_type=jnp.float32,
            ),
            "feat",
            scatter_dimension=0,
            tiled=True,
        )
        + bias2
    ).astype(jnp.bfloat16)
    shard_cot = lax.all_gather(cotangent, "feat", axis=0, tiled=True)
    scale_factor = 1.0 / math.sqrt(shard_nodes * lax.axis_size("node"))
    second_partial = lax.dot_general(
        second_stack, shard_cot, (((1,), (0,)), ((), ())), preferred_element_type=jnp.float32
    )
    second_total = lax.psum(second_partial, "node")
    back_both = lax.dot_general(
        second_weights, shard_cot, (((1,), (1,)), ((), ())), preferred_element_type=jnp.float32
    )
    self_grad = back_both[:hid_part]
    spread = (back_both[hid_part:] / degree_row).astype(jnp.bfloat16)
    spread_blocks = spread.reshape(hid_part, local_blocks, tile_edge)
    contrib = jnp.einsum("wbd,btds->btws", spread_blocks, tiles, preferred_element_type=jnp.float32)
    contrib = contrib.reshape(local_blocks * slot_total, hid_part * tile_edge)
    slot_cols = tile_cols.reshape(-1)
    slot_alive = (
        lax.broadcasted_iota(jnp.int32, tile_cols.shape, 1) < tile_counts[:, None]
    ).reshape(-1)
    total_blocks = local_blocks * lax.axis_size("node")
    targets = lax.broadcasted_iota(jnp.int32, (1, total_blocks), 1)
    selector = ((slot_cols[:, None] == targets) & slot_alive[:, None]).astype(jnp.float32)
    whole_sum = lax.psum(
        lax.dot_general(
            selector,
            contrib,
            (((0,), (0,)), ((), ())),
            precision=lax.Precision.HIGHEST,
            preferred_element_type=jnp.float32,
        ),
        "node",
    )
    back_own = lax.dynamic_slice_in_dim(
        whole_sum, lax.axis_index("node") * local_blocks, local_blocks, 0
    )
    back_cols = (
        back_own.reshape(local_blocks, hid_part, tile_edge)
        .transpose(1, 0, 2)
        .reshape(hid_part, shard_nodes)
    )
    grad_pre = ((self_grad + back_cols) * slope_cols.astype(jnp.float32)).astype(jnp.bfloat16)
    gathered_grad = lax.all_gather(grad_pre, "feat", axis=0, tiled=True)
    first_partial = lax.dot_general(
        first_stack, gathered_grad, (((1,), (1,)), ((), ())), preferred_element_type=jnp.float32
    )
    first_total = lax.psum(first_partial, "node")
    grad_second = (second_total * scale_factor).reshape(2, hid_part, hidden_width)
    grad_first = (first_total * scale_factor).reshape(2, feat_part, hidden_width)
    return (hidden_out, grad_second, grad_first)


def solution(mesh):
    return jax.shard_map(
        shards,
        mesh=mesh,
        in_specs=(
            P("feat", "node"),
            P("node", None),
            P("node"),
            P("node", None, None, None),
            P("node"),
            P(None, "feat", None),
            P(),
            P(None, "feat", None),
            P(),
            P(("node", "feat"), None),
        ),
        out_specs=(P(("node", "feat"), None), P(None, "feat", None), P(None, "feat", None)),
        check_vma=False,
    )
```

profile of v0, /device:TPU:0, one launch (start us, length us, event | category | flops | bytes accessed | tf_op | source)
XLA Modules:
  0.0 626.1 jit_solution(8371738603571695593)
XLA Ops:
  7.2 0.0 all-gather.5.cloned.1.call-start
  7.2 0.7 all-gather.5.cloned.1.call-update
  7.9 0.0 reduce-scatter.3.cloned.1.call-start
  8.0 0.7 convert_element_type.43
  8.7 0.7 compare_select_fusion
  9.4 0.1 copy.34
  9.5 0.1 reshape.107
  9.6 0.7 compare_and_fusion
  10.3 0.1 copy.33
  10.4 0.7 iota_compare_fusion.1
  11.1 49.6 %all-gather.5.cloned.1.call-done = bf16[16,98304]{1,0:T(8,128)(2,1)} async-done(((bf16[16,6144]{1,0:T(8,128)(2,1)}), bf16[16,98304]{1,0:T(8,128)(2,1)}) %all-gather.5.cloned.1.call-update) | async-done | bytes 3145744 | tf_op jit(solution)/shard_map/all_gather | solution.py:33
  60.7 2.4 copy_bitcast_fusion.1
  63.2 3.5 gather_fusion
  66.7 12.1 %fusion.22 = f32[48,2,8,128]{3,2,1,0:T(8,128)S(1)} fusion(bf16[48,16,128,128]{3,2,1,0:T(8,128)(2,1)} %param.13, bf16[48,16,16,128]{3,2,1,0:T(8,128)(2,1)} %bitcast.98, pred[48,16]{1,0:T(8,128)(4,1)S(1)} %copy.33, bf16[48,16]{1,0:T(8,128)(2,1)S(1)} %get-tuple-element.10), kind=kOutput, calls=%fused_computation.24 | convolution fusion | flops 405798912 | bytes 28707072 | tf_op jit(solution)/shard_map/wbts,btds->wbd/dot_general | solution.py:18
  78.8 0.1 fusion.33
  78.9 0.7 copy-done.7
  79.6 3.7 fusion.40
  83.3 0.0 all-gather.9.cloned.1.call-start
  83.4 0.7 all-gather.9.cloned.1.call-update
  84.0 0.0 all-gather.7.cloned.1.call-start
  84.1 40.7 %reduce-scatter.3.cloned.1.call-done = f32[768,256]{1,0:T(8,128)} async-done(((f32[6144,256]{1,0:T(8,128)}), f32[768,256]{1,0:T(8,128)}) %reduce-scatter.3.cloned.1.call-update) | async-done | bytes 786448 | tf_op jit(solution)/shard_map/reduce_scatter | solution.py:41
  124.7 2.2 fusion.38
  126.9 0.2 copy.37
  127.1 11.4 %all_to_all.32 = bf16[8,32,768]{2,1,0:T(8,128)(2,1)S(1)} all-to-all(bf16[8,32,768]{2,1,0:T(8,128)(2,1)S(1)} %bitcast.102), channel_id=1, replica_groups=mesh['feat'=8,'node'=16] {'feat'}, dimensions={0} | all-to-all | bytes 786432 | tf_op jit(solution)/shard_map/all_to_all | solution.py:58
  138.5 0.8 copy.55
  139.3 0.0 all-gather.7.cloned.1.call-update
  139.3 0.0 all-reduce.3.cloned.1.call-start
  139.4 0.1 copy.42
  139.5 0.1 eq.15
  139.5 0.1 lt.46
  139.6 14.3 %all-gather.9.cloned.1.call-done = bf16[6144,256]{1,0:T(8,128)(2,1)} async-done(((bf16[768,256]{1,0:T(8,128)(2,1)}), bf16[6144,256]{1,0:T(8,128)(2,1)}) %all-gather.9.cloned.1.call-update) | async-done | bytes 3145744 | tf_op jit(solution)/shard_map/all_gather | solution.py:82
  154.0 2.9 fusion.48
  156.9 60.5 %all-gather.7.cloned.1.call-done = bf16[32,98304]{1,0:T(8,128)(2,1)} async-done(((bf16[32,6144]{1,0:T(8,128)(2,1)}), bf16[32,98304]{1,0:T(8,128)(2,1)}) %all-gather.7.cloned.1.call-update) | async-done | bytes 6291472 | tf_op jit(solution)/shard_map/all_gather | solution.py:61
  217.4 6.5 %copy_bitcast_fusion = bf16[32,768,128]{2,0,1:T(8,128)(2,1)} fusion(bf16[32,98304]{1,0:T(8,128)(2,1)} %all-gather.7.cloned.1.call-done), kind=kLoop, calls=%fused_computation.5 | loop fusion | bytes 12582912 | tf_op jit(solution)/shard_map/reshape | solution.py:12
  223.9 7.9 %gather_fusion.1 = bf16[768,32,128]{2,1,0:T(8,128)(2,1)} fusion(bf16[32,768,128]{2,0,1:T(8,128)(2,1)} %copy_bitcast_fusion, s32[1024]{0:T(1024)S(1)} %pad_clamp_fusion), kind=kCustom, calls=%fused_computation.1 | custom fusion | bytes 12585984 | tf_op jit(solution)/shard_map/jit(_take)/gather | solution.py:13
  231.8 14.0 %fusion.19 = f32[48,4,8,128]{3,2,1,0:T(8,128)S(1)} fusion(bf16[48,16,128,128]{3,2,1,0:T(8,128)(2,1)} %param.13, bf16[48,16,32,128]{3,2,1,0:T(8,128)(2,1)} %bitcast.97, pred[48,16]{1,0:T(8,128)(4,1)S(1)} %copy.33, bf16[48,16]{1,0:T(8,128)(2,1)S(1)} %get-tuple-element.10), kind=kOutput, calls=%fused_computation.23 | convolution fusion | flops 811597824 | bytes 32246016 | tf_op jit(solution)/shard_map/wbts,btds->wbd/dot_general | solution.py:18
  245.8 1.0 fusion.36
  246.8 0.1 copy.59
  246.9 10.0 %fusion.34 = f32[48,32,16,128]{3,1,2,0:T(8,128)S(1)} fusion(bf16[48,16,128,128]{3,2,1,0:T(8,128)(2,1)} %param.13, bf16[32,48,128,1]{2,1,0,3:T(8,128)(2,1)S(1)} %bitcast.101), kind=kOutput, calls=%fused_computation.46 | convolution fusion | flops 805306368 | bytes 38141952 | tf_op jit(solution)/shard_map/wbd,btds->btws/dot_general | solution.py:94
  256.9 29.1 %fusion = f32[768,4096]{1,0:T(8,128)} fusion(f32[96,8,32,128]{3,2,1,0:T(8,128)S(1)} %bitcast.93, s32[768]{0:T(1024)S(1)} %eq.15, pred[768]{0:T(1024)(128)(4,1)S(1)} %lt.46), kind=kOutput, calls=%fused_computation.2 | convolution fusion | flops 28992208896 | bytes 25169664 | tf_op jit(solution)/shard_map/dot_general | solution.py:104
  285.9 1.3 fusion.31
  287.2 0.3 reduce-scatter.5.cloned.1.call-start
  287.5 0.7 copy-done.4
  288.2 3.7 fusion.32
  291.9 0.0 reduce-scatter.5.cloned.1.call-update
  291.9 1.0 copy-done.8
  292.9 0.9 copy.45
  293.8 4.3 all-to-all-start.1
  298.1 0.0 all-gather.11.cloned.1.call-start
  298.2 8.9 %all-to-all-done.1 = bf16[8,32,768]{2,1,0:T(8,128)(2,1)S(1)} async-done(((bf16[8,32,768]{2,1,0:T(8,128)(2,1)}), bf16[8,32,768]{2,1,0:T(8,128)(2,1)S(1)}, u32[]{:S(2)}, u32[]{:S(2)}) %all-to-all-start.1) | async-done | bytes 393248 | tf_op jit(solution)/shard_map/all_to_all | solution.py:59
  307.1 0.1 convert_bitcast_fusion
  307.1 0.1 copy.58
  307.2 160.0 %all-reduce.3.cloned.1.call-done = (f32[64,256]{1,0:T(8,128)}, f32[768,4096]{1,0:T(8,128)}) async-done(((f32[64,256]{1,0:T(8,128)}, f32[768,4096]{1,0:T(8,128)}), (f32[64,256]{1,0:T(8,128)}, f32[768,4096]{1,0:T(8,128)})) %all-reduce.3.cloned.1.call-update) | async-done | bytes 12648464 | tf_op jit(solution)/shard_map/psum | solution.py:87
  467.2 1.2 dynamic-slice_bitcast_fusion
  468.4 0.1 copy.61
  468.5 0.9 fusion.28
  469.4 0.0 all-gather.11.cloned.1.call-update
  469.4 42.3 %reduce-scatter.5.cloned.1.call-done = f32[768,256]{1,0:T(8,128)} async-done(((f32[6144,256]{1,0:T(8,128)}), f32[768,256]{1,0:T(8,128)}) %reduce-scatter.5.cloned.1.call-update) | async-done | bytes 786448 | tf_op jit(solution)/shard_map/reduce_scatter | solution.py:69
  511.7 1.9 add_convert_fusion
  513.7 0.6 broadcast_multiply_fusion
  514.3 26.7 %all-gather.11.cloned.1.call-done = bf16[256,6144]{1,0:T(8,128)(2,1)} async-done(((bf16[32,6144]{1,0:T(8,128)(2,1)}), bf16[256,6144]{1,0:T(8,128)(2,1)}) %all-gather.11.cloned.1.call-update) | async-done | bytes 3145744 | tf_op jit(solution)/shard_map/all_gather | solution.py:122
  541.1 3.1 fusion.39
  544.1 74.5 %psum.23 = f32[32,256]{1,0:T(8,128)S(1)} all-reduce(f32[32,256]{1,0:T(8,128)S(1)} %fusion.39), channel_id=1, replica_groups=mesh['feat'=8,'node'=16] {'node'}, use_global_device_ids=true, to_apply=%region_4.5 | all-reduce | flops 8192 | bytes 65536 | tf_op jit(solution)/shard_map/psum | solution.py:126
  618.6 0.6 broadcast_multiply_fusion.1
  (28 shorter events, 0.1 us)
Async XLA Ops:
  7.2 146.8 %copy-start = (bf16[2,32,256]{2,1,0:T(8,128)(2,1)S(1)}, bf16[2,32,256]{2,1,0:T(8,128)(2,1)}, u32[]{:S(2)}) copy-start(bf16[2,32,256]{2,1,0:T(8,128)(2,1)} %param.17) | copy-start | bytes 98308
  7.2 53.5 %all-gather.5.cloned.1.call-start = ((), (), s32[]{:S(2)}) async-start(), calls=%async_computation.4 | async-start | bytes 3342336 | tf_op jit(solution)/shard_map/all_gather | solution.py:33
  7.9 116.8 %reduce-scatter.3.cloned.1.call-start = ((), (), s32[]{:S(2)}) async-start(), calls=%async_computation.5 | async-start | bytes 7077888 | tf_op jit(solution)/shard_map/reduce_scatter | solution.py:41
  66.7 12.9 %copy-start.5 = (bf16[16,6144]{1,0:T(8,128)(2,1)S(1)}, bf16[16,6144]{1,0:T(8,128)(2,1)}, u32[]{:S(2)}) copy-start(bf16[16,6144]{1,0:T(8,128)(2,1)} %param.10) | copy-start | bytes 589828
  66.7 12.9 %copy-start.11 = (bf16[2,16,256]{2,1,0:T(8,128)(2,1)S(1)}, bf16[2,16,256]{2,1,0:T(8,128)(2,1)}, u32[]{:S(2)}) copy-start(bf16[2,16,256]{2,1,0:T(8,128)(2,1)} %param.15) | copy-start | bytes 49156
  78.9 0.7 copy-start.7
  83.3 41.5 %copy-start.12 = (f32[256]{0:T(256)S(1)}, f32[256]{0:T(256)}, u32[]{:S(2)}) copy-start(f32[256]{0:T(256)} %param.16) | copy-start | bytes 3076
  83.3 56.1 %copy-start.9 = (s32[48,16]{0,1:T(8,128)S(1)}, s32[48,16]{0,1:T(8,128)}, u32[]{:S(2)}) copy-start(s32[48,16]{0,1:T(8,128)} %param.11) | copy-start | bytes 9220
  83.3 70.6 %all-gather.9.cloned.1.call-start = ((), (), s32[]{:S(2)}) async-start(), calls=%async_computation.8 | async-start | bytes 3538944 | tf_op jit(solution)/shard_map/all_gather | solution.py:82
  84.0 133.4 %all-gather.7.cloned.1.call-start = ((), (), s32[]{:S(2)}) async-start(), calls=%async_computation.6 | async-start | bytes 6684672 | tf_op jit(solution)/shard_map/all_gather | solution.py:61
  139.3 327.8 %all-reduce.3.cloned.1.call-start = ((), (), s32[]{:S(2)}) async-start(), calls=%async_computation.10 | async-start | bytes 25296896 | tf_op jit(solution)/shard_map/psum | solution.py:87
  256.8 29.1 %copy-start.1 = (bf16[6144,256]{1,0:T(8,128)(2,1)S(1)}, bf16[6144,256]{1,0:T(8,128)(2,1)}, u32[]{:S(2)}) copy-start(bf16[6144,256]{1,0:T(8,128)(2,1)} %all-gather.9.cloned.1.call-done) | copy-start | bytes 9437188
  256.8 29.1 %copy-start.2 = (bf16[8,4,8,768]{3,2,0,1:T(8,128)(2,1)S(1)}, bf16[8,4,8,768]{3,2,0,1:T(8,128)(2,1)}, u32[]{:S(2)}) copy-start(bf16[8,4,8,768]{3,2,0,1:T(8,128)(2,1)} %copy.55) | copy-start | bytes 1179652
  256.8 29.1 %copy-start.3 = (bf16[32,6144]{1,0:T(8,128)(2,1)S(1)}, bf16[32,6144]{1,0:T(8,128)(2,1)}, u32[]{:S(2)}) copy-start(bf16[32,6144]{1,0:T(8,128)(2,1)} %get-tuple-element.8) | copy-start | bytes 1179652
  287.2 1.0 copy-start.4
  287.2 224.5 %reduce-scatter.5.cloned.1.call-start = ((), (), s32[]{:S(2)}) async-start(), calls=%async_computation.7 | async-start | bytes 7077888 | tf_op jit(solution)/shard_map/reduce_scatter | solution.py:69
  291.9 1.0 copy-start.8
  293.8 13.2 %all-to-all-start.1 = ((bf16[8,32,768]{2,1,0:T(8,128)(2,1)}), bf16[8,32,768]{2,1,0:T(8,128)(2,1)S(1)}, u32[]{:S(2)}, u32[]{:S(2)}) async-start(bf16[8,32,768]{2,1,0:T(8,128)(2,1)} %bitcast.20), calls=%async_computation.3 | async-start | bytes 786432 | tf_op jit(solution)/shard_map/all_to_all | solution.py:59
  298.1 243.0 %all-gather.11.cloned.1.call-start = ((), (), s32[]{:S(2)}) async-start(), calls=%async_computation.9 | async-start | bytes 3538944 | tf_op jit(solution)/shard_map/all_gather | solution.py:122
  467.1 44.6 %copy-start.13 = (f32[256]{0:T(256)S(1)}, f32[256]{0:T(256)}, u32[]{:S(2)}) copy-start(f32[256]{0:T(256)} %param.18) | copy-start | bytes 3076
  468.4 45.3 %copy-start.10 = (f32[64,256]{1,0:T(8,128)S(1)}, f32[64,256]{1,0:T(8,128)}, u32[]{:S(2)}) copy-start(f32[64,256]{1,0:T(8,128)} %get-tuple-element.3) | copy-start | bytes 196612
  468.4 72.7 %copy-start.6 = (bf16[16,6144]{1,0:T(8,128)(2,1)S(1)}, bf16[16,6144]{1,0:T(8,128)(2,1)}, u32[]{:S(2)}) copy-start(bf16[16,6144]{1,0:T(8,128)(2,1)} %param.10) | copy-start | bytes 589828
Sparse Core Ops, SparseCore 0:
  10.2 50.5 all-gather.4
  83.4 41.2 reduce-scatter.2
  126.4 27.4 all-gather.8
  155.9 61.4 all-gather.6
  287.4 179.7 all-reduce.2
  469.5 42.1 reduce-scatter.4
  513.5 27.4 all-gather.10
where the time goes:
time: 627 us; the launch traced here: 626 us
  waiting for transfers between devices  404 us (64%)
  blocking collectives  85.9 us (14%)
  matrix products  79.8 us (13%)
  local copies, waits for them, and re-layouts  26.6 us (4%)
  between operations  14.3 us (2%)
  other arithmetic  10.2 us (2%)
    psum x1, waiting for transfers between devices, shards(): second_total = lax.psum(second_partial, 'node')  160 us
    psum x1, blocking collectives, shards(): first_total = lax.psum(first_partial, 'node')  74.5 us
    all_gather x1, waiting for transfers between devices, shards(): all_hidden = lax.all_gather(hidden_cols, 'node', axis=1, tiled=True)  60.5 us
    all_gather x1, waiting for transfers between devices, shards(): all_feats = lax.all_gather(features, 'node', axis=1, tiled=True)  49.6 us
    reduce_scatter x1, waiting for transfers between devices, shards(): lax.psum_scatter(lax.dot_general(picked_cols, second_weights, (((0,), (0,...  42.3 us
    reduce_scatter x1, waiting for transfers between devices, shards(): lax.psum_scatter(lax.dot_general(picked_cols, first_weights, (((0,), (0,)...  40.7 us
    dot_general x1, matrix products, shards(): lax.dot_general(selector, contrib, (((0,), (0,)), ((), ())), precision=la...  29.1 us
    all_gather x1, waiting for transfers between devices, shards(): gathered_grad = lax.all_gather(grad_pre, 'feat', axis=0, tiled=True)  26.7 us
  transfers between devices with their start and end apart: 8, of which 8 were waited for; matrix products, arithmetic and copies ran while one was open for 3% of the time, Pallas kernels for 0%

commit v1 on v0

v1 whole, which is shorter than its diff:
```python
import functools
import math

import jax
import jax.numpy as jnp
from jax import lax
from jax.experimental import pallas as pl
from jax.experimental.pallas import tpu as pltpu
from jax.sharding import PartitionSpec as P

MESH = pl.DeviceIdType.MESH
BF16 = jnp.bfloat16
F32 = jnp.float32
FEATS = 8
SIDE = 4
BLK = 128
NB = 48
OWN = NB // FEATS
HALF, QUARTER = NB // 2, NB // 4
GROUP = 4
BATCH = 4
STAGES = 4
AHEAD = (0, -1, 1, 2)
VMEM = pl.BlockSpec(memory_space=pltpu.VMEM)
SMEM = pl.BlockSpec(memory_space=pltpu.SMEM)
ANY = pl.BlockSpec(memory_space=pl.ANY)


def dot(left, right, dims):
    return lax.dot_general(left, right, (dims, ((), ())), preferred_element_type=F32)


class Place:
    def __init__(self):
        self.feat = lax.axis_index("feat")
        self.node = lax.axis_index("node")
        self.x = self.node // SIDE
        self.z = self.node % SIDE

    def peer(self, step):
        return (self.feat + step) % FEATS

    def shift(self, dx, dz):
        return ((self.x + dx + SIDE) % SIDE) * SIDE + (self.z + dz + SIDE) % SIDE

    def turned(self, half, first, second):
        return self.shift(first, second) if half == 0 else self.shift(second, first)

    def greet(self, far):
        barrier = pltpu.get_barrier_semaphore()
        steps = (1, 2, 3) if far else (1, 3)
        others = [{"feat": self.peer(step)} for step in range(1, FEATS)]
        others += [{"node": self.shift(step, 0)} for step in steps]
        others += [{"node": self.shift(0, step)} for step in steps]
        for other in others:
            pl.semaphore_signal(barrier, inc=1, device_id=other, device_id_type=MESH)
        pl.semaphore_wait(barrier, len(others))


class Copies:
    def __init__(self):
        self.sent = []

    def send(self, source, target, send_sem, recv_sem, device):
        copy = pltpu.make_async_remote_copy(
            src_ref=source,
            dst_ref=target,
            send_sem=send_sem,
            recv_sem=recv_sem,
            device_id=device,
            device_id_type=MESH,
        )
        copy.start()
        self.sent.append(copy)
        return copy

    def finish(self):
        for copy in self.sent:
            copy.wait_send()


class Regroup:
    def __init__(self, copies, place, source_at, target_at, send_sems, recv_sems):
        self.place, self.source_at, self.target_at = place, source_at, target_at
        self.parts = []
        for step in range(1, FEATS):
            to = place.peer(step)
            self.parts.append(
                copies.send(
                    source_at(to),
                    target_at(place.feat),
                    send_sems.at[step - 1],
                    recv_sems.at[step - 1],
                    {"feat": to},
                )
            )
        target_at(place.feat)[...] = source_at(place.feat)[...]

    def wait(self):
        for part in self.parts:
            part.wait_recv()


class Gather:
    def __init__(self, copies, place, own, out, send_sems, recv_sems):
        self.copies, self.place, self.own, self.out = copies, place, own, out
        self.send_sems, self.recv_sems = send_sems, recv_sems
        self.made = {}

    def _send(self, half, unit, role, source, target, first, second):
        place = self.place
        self.made[half, unit, role] = self.copies.send(
            source,
            target,
            self.send_sems.at[half, unit, role],
            self.recv_sems.at[half, unit, role],
            {"node": place.turned(half, first, second)},
        )

    def full(self, half, unit):
        rows = pl.ds(half * HALF, HALF)
        ahead = 0 if unit == SIDE else AHEAD[unit]
        shard = self.place.turned(half, ahead, 0)
        source = self.own.at[rows] if ahead == 0 else self.out.at[shard, rows]
        for role, way in ((0, 1), (1, -1)):
            move = (way, 0) if unit == SIDE else (0, way)
            self._send(half, unit, role, source, self.out.at[shard, rows], *move)

    def forward(self, half, unit, role):
        way = 1 if role == 0 else -1
        self.made[half, unit, role].wait_recv()
        rows = pl.ds(half * HALF + role * QUARTER, QUARTER)
        if unit == SIDE:
            shard, move = self.place.turned(half, -way, 0), (way, 0)
        else:
            shard, move = self.place.turned(half, AHEAD[unit], -way), (0, way)
        part = self.out.at[shard, rows]
        self._send(half, unit, role + 2, part, part, *move)

    def arrived(self, half, unit):
        for role in (2, 3):
            self.made[half, unit, role].wait_recv()

    def start(self):
        for half in range(2):
            self.full(half, SIDE)
        for half in range(2):
            self.full(half, 0)

    def rows(self):
        for role in range(2):
            for half in range(2):
                self.forward(half, SIDE, role)
                self.full(half, role + 1)

    def near(self):
        for role in range(2):
            for half in range(2):
                self.forward(half, 0, role)
        for half in range(2):
            self.arrived(half, SIDE)
            self.full(half, 3)

    def far(self):
        for unit in range(1, SIDE):
            for role in range(2):
                for half in range(2):
                    self.forward(half, unit, role)

    def last(self):
        for unit in range(SIDE):
            for half in range(2):
                self.arrived(half, unit)


class Scatter:
    def __init__(self, copies, place, parts, bufs, send_sems, recv_sems):
        self.copies, self.place, self.parts = copies, place, parts
        self.pass1, self.got1, self.sum1, self.half1, self.pass2, self.got2, self.sum2 = bufs
        self.send_sems, self.recv_sems = send_sems, recv_sems
        self.made = {}

    def _send(self, half, phase, side, kind, source, target):
        way = 1 if side == 0 else -1
        first, second = (way, 0) if phase == 0 else (0, way)
        self.made[half, phase, side, kind] = self.copies.send(
            source,
            target,
            self.send_sems.at[half, phase, side, kind],
            self.recv_sems.at[half, phase, side, kind],
            {"node": self.place.turned(half, first, second)},
        )

    def _line(self, half, ahead, quarter=None):
        rows = pl.ds(half * HALF, HALF)
        if quarter is not None:
            rows = pl.ds(half * HALF + quarter * QUARTER, QUARTER)
        if half == 0:
            return self.parts.at[(self.place.x + ahead + SIDE) % SIDE, :, rows]
        return self.parts.at[:, (self.place.z + ahead + SIDE) % SIDE, rows]

    def _unit(self, half, ahead, quarter):
        at = self.place.z if half == 0 else self.place.x
        rows = pl.ds(quarter * QUARTER, QUARTER)
        return self.half1.at[half, (at + ahead + SIDE) % SIDE, rows]

    def start(self):
        for half in range(2):
            for side, way in ((0, 1), (1, -1)):
                self._send(half, 0, side, 0, self._line(half, 2 * way, side), self.pass1.at[half, side])
        for half in range(2):
            for side, way in ((0, 1), (1, -1)):
                rows = pl.ds((1 - side) * QUARTER, QUARTER)
                self._send(half, 0, side, 1, self._line(half, way, 1 - side), self.got1.at[half, side, :, rows])

    def middle(self):
        for side, way in ((0, 1), (1, -1)):
            for half in range(2):
                self.made[half, 0, side, 0].wait_recv()
                mine, came, total = self._line(half, way, side), self.pass1.at[half, side], self.sum1.at[half, side]

                @pl.loop(0, SIDE)
                def _(shard):
                    total[shard] = (mine[shard].astype(F32) + came[shard].astype(F32)).astype(BF16)

                rows = pl.ds(side * QUARTER, QUARTER)
                self._send(half, 0, side, 2, total, self.got1.at[half, side, :, rows])

    def turn(self):
        for half in range(2):
            for side in range(2):
                for kind in (1, 2):
                    self.made[half, 0, side, kind].wait_recv()
            mine, left, right, total = self._line(half, 0), self.got1.at[half, 0], self.got1.at[half, 1], self.half1.at[half]

            @pl.loop(0, SIDE)
            def _(shard):
                near = left[shard].astype(F32) + right[shard].astype(F32)
                total[shard] = (mine[shard].astype(F32) + near).astype(BF16)

            for side, way in ((0, 1), (1, -1)):
                self._send(half, 1, side, 0, self._unit(half, 2 * way, side), self.pass2.at[half, side])
            for side, way in ((0, 1), (1, -1)):
                rows = pl.ds((1 - side) * QUARTER, QUARTER)
                self._send(half, 1, side, 1, self._unit(half, way, 1 - side), self.got2.at[half, side, rows])

    def middle2(self):
        for side, way in ((0, 1), (1, -1)):
            for half in range(2):
                self.made[half, 1, side, 0].wait_recv()
                total = self.sum2.at[half, side]
                mine, came = self._unit(half, way, side)[...], self.pass2[half, side]
                total[...] = (mine.astype(F32) + came.astype(F32)).astype(BF16)
                rows = pl.ds(side * QUARTER, QUARTER)
                self._send(half, 1, side, 2, total, self.got2.at[half, side, rows])

    def end(self, out):
        for half in range(2):
            for side in range(2):
                for kind in (1, 2):
                    self.made[half, 1, side, kind].wait_recv()
            for quarter in range(2):
                rows = pl.ds(quarter * QUARTER, QUARTER)
                near = self.got2[half, 0, rows].astype(F32) + self.got2[half, 1, rows].astype(F32)
                total = self._unit(half, 0, quarter)[...].astype(F32) + near
                out[pl.ds(half * HALF + quarter * QUARTER, QUARTER)] = total.astype(BF16)


class Total:
    def __init__(self, copies, place, part, feat_buf, x_buf, z_buf, send_sems, recv_sems):
        self.copies, self.place, self.part = copies, place, part
        self.bufs = (feat_buf, x_buf, z_buf)
        self.sems = (send_sems, recv_sems)

    def over_feat(self):
        buf = self.bufs[0]
        sends, recvs = self.sems
        self.regroup = Regroup(
            self.copies,
            self.place,
            lambda to: self.part.at[to],
            lambda slot: buf.at[slot],
            sends.at[pl.ds(0, FEATS - 1)],
            recvs.at[pl.ds(0, FEATS - 1)],
        )

    def _spread(self, axis, value):
        buf, place = self.bufs[1 + axis], self.place
        sends, recvs = self.sems
        at = place.x if axis == 0 else place.z
        buf[at] = value
        self.parts = []
        for step in range(1, SIDE):
            slot = FEATS - 1 + axis * (SIDE - 1) + step - 1
            to = place.shift(step, 0) if axis == 0 else place.shift(0, step)
            self.parts.append(
                self.copies.send(buf.at[at], buf.at[at], sends.at[slot], recvs.at[slot], {"node": to})
            )

    def over_x(self):
        self.regroup.wait()
        self._spread(0, sum(self.bufs[0][slot] for slot in range(FEATS)))

    def over_z(self):
        for part in self.parts:
            part.wait_recv()
        self._spread(1, sum(self.bufs[1][slot] for slot in range(SIDE)))

    def end(self):
        for part in self.parts:
            part.wait_recv()
        return sum(self.bufs[2][slot] for slot in range(SIDE))


def own_rows(feat):
    return pl.ds(feat * OWN, OWN)


def gather_kernel(
    features, weights1, weights2, cotangent, degrees,
    all_feats, own_feats, all_weights1, all_weights2, spread,
    blocks, outgoing, gather_send, gather_recv, feat_send, feat_recv, local_sem,
):
    place, copies = Place(), Copies()
    place.greet(False)
    regroups = [
        Regroup(
            copies, place, lambda to: weights, lambda slot: target.at[slot], feat_send.at[number], feat_recv.at[number]
        )
        for number, (weights, target) in enumerate(((weights2, all_weights2), (weights1, all_weights1)))
    ]
    for block in range(NB):
        blocks[block] = features[:, block * BLK : (block + 1) * BLK]
    gather = Gather(copies, place, blocks, all_feats, gather_send, gather_recv)
    gather.start()
    own = pltpu.make_async_copy(blocks, all_feats.at[place.node], local_sem)
    own.start()
    regroups.append(
        Regroup(
            copies, place, lambda to: blocks.at[own_rows(to)], lambda slot: own_feats.at[slot], feat_send.at[2], feat_recv.at[2]
        )
    )
    gather.rows()
    regroups[0].wait()
    neighbour = all_weights2[:, 1].reshape(-1, all_weights2.shape[-1])
    for block in range(OWN):
        nodes = cotangent[block * BLK : (block + 1) * BLK, :]
        back = dot(neighbour, nodes, ((1,), (1,)))
        degree = degrees[pl.ds(place.feat * OWN + block, 1), :].astype(F32)
        outgoing[:, block] = (back / degree).astype(BF16).reshape(FEATS, -1, BLK)
    regroups.append(
        Regroup(
            copies, place, lambda to: outgoing.at[to], lambda slot: spread.at[slot], feat_send.at[3], feat_recv.at[3]
        )
    )
    gather.near()
    gather.far()
    for regroup in regroups[1:]:
        regroup.wait()
    gather.last()
    own.wait()
    copies.finish()


def plan_groups(counts, groups):
    def row(block, total):
        for part in range(4):
            groups[total + part] = block * 4 + part
        return total + (counts[block] + GROUP - 1) // GROUP

    total = lax.fori_loop(0, NB, row, jnp.int32(0))
    for part in range(BATCH):
        groups[total + part] = 0
    return total


def each_step(counts, groups, tiles, held, tile_sems, work):
    total = plan_groups(counts, groups)
    steps = (total + BATCH - 1) // BATCH

    def copy(step, place):
        slot = step % STAGES
        group = groups[step * BATCH + place]
        return pltpu.make_async_copy(tiles.at[group], held.at[slot, place], tile_sems.at[slot, place])

    def fetch(step):
        @pl.when(step < steps)
        def _():
            for place in range(BATCH):
                copy(step, place).start()

    for step in range(STAGES - 1):
        fetch(step)

    def body(step, carry):
        fetch(step + STAGES - 1)
        entries = []
        for place in range(BATCH):
            copy(step, place).wait()
            group = groups[step * BATCH + place]
            block, first = group // 4, (group % 4) * GROUP
            live = jnp.where(step * BATCH + place < total, counts[block], 0)
            wide = jnp.concatenate([held[step % STAGES, place, slot] for slot in range(GROUP)], axis=1)
            entries.append((block, first, live, wide))
        work(entries)
        return carry

    lax.fori_loop(0, steps, body, jnp.int32(0))


def picked(source, cols, entry):
    block, first, live, wide = entry
    parts = []
    for slot in range(GROUP):
        value = source[cols[block, first + slot]]
        parts.append(jnp.where(first + slot < live, value, jnp.zeros_like(value)))
    return dot(jnp.concatenate(parts, axis=1), wide, ((1,), (1,)))


def write_mean(sums, degrees, mean):
    @pl.loop(0, NB)
    def _(block):
        mean[block] = (sums[block] / degrees[pl.ds(block, 1), :].astype(F32)).astype(BF16)


def both_kernel(cols, counts, tiles, source, spread, degrees, mean, back, held, sums, back_sums, groups, tile_sems):
    sums[...] = jnp.zeros_like(sums)

    @pl.loop(0, back_sums.shape[0] // 16)
    def _(part):
        rows = pl.ds(part * 16, 16)
        back_sums[rows] = jnp.zeros((16,) + back_sums.shape[1:], F32)

    def work(entries):
        products = [picked(source, cols, entry) for entry in entries]
        backs = [dot(spread[entry[0]], entry[3], ((1,), (0,))) for entry in entries]
        for entry, product in zip(entries, products):
            sums[entry[0]] += product
        for (block, first, live, _), product in zip(entries, backs):
            for slot in range(GROUP):
                part = product[:, slot * BLK : (slot + 1) * BLK]
                back_sums[cols[block, first + slot]] += jnp.where(first + slot < live, part, jnp.zeros_like(part))

    each_step(counts, groups, tiles, held, tile_sems, work)
    write_mean(sums, degrees, mean)

    @pl.loop(0, back_sums.shape[0] // 16)
    def _(part):
        rows = pl.ds(part * 16, 16)
        back[rows] = back_sums[rows].astype(BF16)


def mean_kernel(cols, counts, tiles, source, degrees, mean, held, sums, groups, tile_sems):
    sums[...] = jnp.zeros_like(sums)

    def work(entries):
        products = [picked(source, cols, entry) for entry in entries]
        for entry, product in zip(entries, products):
            sums[entry[0]] += product

    each_step(counts, groups, tiles, held, tile_sems, work)
    write_mean(sums, degrees, mean)


def middle_kernel(
    scale, feat_mean, back_parts, own_feats, weights1, bias1, weights2, cotangent,
    all_hidden, hidden, grad_first,
    means, slopes, own_hidden, back, own_back, grads, feat_buf, x_buf, z_buf, bufs,
    gather_send, gather_recv, scatter_send, scatter_recv, feat_send, feat_recv, total_send, total_recv, local_sem,
):
    place, copies = Place(), Copies()
    place.greet(True)
    to_means = Regroup(
        copies, place, lambda to: feat_mean.at[own_rows(to)], lambda slot: means.at[slot], feat_send.at[0], feat_recv.at[0]
    )
    scatter = Scatter(copies, place, back_parts, bufs, scatter_send, scatter_recv)
    scatter.start()
    width = weights1.shape[-1]
    first = weights1[...].reshape(-1, width)
    to_means.wait()

    def stack(block):
        parts = []
        for part in range(FEATS):
            parts += [own_feats[part, block], means[part, block]]
        return jnp.concatenate(parts, axis=0)

    for block in range(OWN):
        pre = dot(first, stack(block), ((0,), (0,))) + bias1[...]
        sigmoid = jax.nn.sigmoid(pre)
        slopes[block] = (sigmoid * (1.0 + pre * (1.0 - sigmoid))).astype(BF16)
        hidden[:, block] = (pre * sigmoid).astype(BF16).reshape(FEATS, -1, BLK)
    to_hidden = Regroup(
        copies, place, lambda to: hidden.at[to], lambda slot: own_hidden.at[own_rows(slot)], feat_send.at[1], feat_recv.at[1]
    )
    scatter.middle()
    to_hidden.wait()
    gather = Gather(copies, place, own_hidden, all_hidden, gather_send, gather_recv)
    own = pltpu.make_async_copy(own_hidden, all_hidden.at[place.node], local_sem)
    own.start()
    scatter.turn()
    gather.start()
    scatter.middle2()
    gather.rows()
    scatter.end(back)
    to_back = Regroup(
        copies, place, lambda to: back.at[own_rows(to)], lambda slot: own_back.at[slot], feat_send.at[2], feat_recv.at[2]
    )
    gather.near()
    to_back.wait()
    own_weights = weights2[:, 0].reshape(-1, weights2.shape[-1])
    total = None
    for block in range(OWN):
        nodes = cotangent[block * BLK : (block + 1) * BLK, :]
        came = jnp.concatenate([own_back[part, block] for part in range(FEATS)], axis=0)
        grad = dot(own_weights, nodes, ((1,), (1,))) + came.astype(F32)
        grad = (grad * slopes[block].astype(F32)).astype(BF16)
        product = dot(stack(block), grad, ((1,), (1,)))
        total = product if total is None else total + product
    grads[...] = total.reshape(grads.shape)
    summed = Total(copies, place, grads, feat_buf, x_buf, z_buf, total_send, total_recv)
    summed.over_feat()
    gather.far()
    summed.over_x()
    summed.over_z()
    grad_first[...] = summed.end() * scale
    gather.last()
    own.wait()
    copies.finish()


def last_kernel(
    scale, hidden_mean, hidden, weights2, bias2, cotangent,
    hidden_out, grad_second,
    means, grads, feat_buf, x_buf, z_buf, feat_send, feat_recv, total_send, total_recv,
):
    place, copies = Place(), Copies()
    place.greet(True)
    to_means = Regroup(
        copies, place, lambda to: hidden_mean.at[own_rows(to)], lambda slot: means.at[slot], feat_send, feat_recv
    )
    second = weights2[...].reshape(-1, weights2.shape[-1])
    to_means.wait()

    def stack(block):
        parts = []
        for part in range(FEATS):
            parts += [hidden[part, block], means[part, block]]
        return jnp.concatenate(parts, axis=0)

    total = None
    for block in range(OWN):
        nodes = cotangent[block * BLK : (block + 1) * BLK, :]
        product = dot(stack(block), nodes, ((1,), (0,)))
        total = product if total is None else total + product
    grads[...] = total.reshape(grads.shape)
    summed = Total(copies, place, grads, feat_buf, x_buf, z_buf, total_send, total_recv)
    summed.over_feat()
    for block in range(OWN):
        out = dot(stack(block), second, ((0,), (0,))) + bias2[...]
        hidden_out[block * BLK : (block + 1) * BLK, :] = out.astype(BF16)
    summed.over_x()
    summed.over_z()
    grad_second[...] = summed.end() * scale
    copies.finish()


def remote(collective_id):
    return pltpu.CompilerParams(
        collective_id=collective_id, has_side_effects=True, vmem_limit_bytes=44 * 1024 * 1024
    )


def shape(*dims, dtype=BF16):
    return jax.ShapeDtypeStruct(dims, dtype)


def buf(*dims, dtype=BF16):
    return pltpu.VMEM(dims, dtype)


def dma(*dims):
    return pltpu.SemaphoreType.DMA(dims)


def shards(
    features, tile_cols, tile_counts, tiles, degrees, weights1, bias1, weights2, bias2, cotangent
):
    feat_part = features.shape[0]
    hid_part = weights2.shape[1]
    width = weights2.shape[2]
    shard_total = lax.axis_size("node")
    block_total = shard_total * NB
    scale = 1.0 / math.sqrt(features.shape[1] * shard_total)
    own_nodes = OWN * BLK
    degree_rows = degrees.reshape(NB, BLK)
    groups = tiles.reshape(NB * tiles.shape[1] // GROUP, GROUP, BLK, BLK)

    all_feats, own_feats, all_weights1, all_weights2, spread = pl.pallas_call(
        gather_kernel,
        out_shape=(
            shape(shard_total, NB, feat_part, BLK),
            shape(FEATS, OWN, feat_part, BLK),
            shape(FEATS, 2, feat_part, width),
            shape(FEATS, 2, hid_part, width),
            shape(FEATS, OWN, hid_part, BLK),
        ),
        in_specs=[VMEM] * 5,
        out_specs=(ANY, VMEM, VMEM, VMEM, VMEM),
        scratch_shapes=[
            buf(NB, feat_part, BLK),
            buf(FEATS, OWN, hid_part, BLK),
            dma(2, 5, 4),
            dma(2, 5, 4),
            dma(4, FEATS - 1),
            dma(4, FEATS - 1),
            pltpu.SemaphoreType.DMA,
        ],
        compiler_params=remote(1),
        name="gather_features",
    )(features, weights1, weights2, cotangent, degree_rows)

    held = buf(STAGES, BATCH, GROUP, BLK, BLK)
    listed = pltpu.SMEM((NB * 4 + 2 * BATCH,), jnp.int32)
    plain = pltpu.CompilerParams(vmem_limit_bytes=52 * 1024 * 1024)
    feat_mean, back_parts = pl.pallas_call(
        both_kernel,
        out_shape=(shape(NB, feat_part, BLK), shape(block_total, hid_part, BLK)),
        in_specs=[SMEM, SMEM, ANY, VMEM, VMEM, VMEM],
        out_specs=(VMEM, VMEM),
        scratch_shapes=[
            held,
            buf(NB, feat_part, BLK, dtype=F32),
            buf(block_total, hid_part, BLK, dtype=F32),
            listed,
            dma(STAGES, BATCH),
        ],
        compiler_params=plain,
        name="aggregate_both",
    )(
        tile_cols,
        tile_counts,
        groups,
        all_feats.reshape(block_total, feat_part, BLK),
        spread.reshape(NB, hid_part, BLK),
        degree_rows,
    )

    row = (SIDE, HALF, hid_part, BLK)
    part_row = (SIDE, QUARTER, hid_part, BLK)
    middle_bufs = (
        buf(2, 2, *part_row),
        buf(2, 2, *row),
        buf(2, 2, *part_row),
        buf(2, *row),
        buf(2, 2, *part_row[1:]),
        buf(2, 2, *row[1:]),
        buf(2, 2, *part_row[1:]),
    )
    first_rows = 2 * feat_part
    all_hidden, hidden, grad_first = pl.pallas_call(
        functools.partial(middle_kernel, scale),
        out_shape=(
            shape(shard_total, NB, hid_part, BLK),
            shape(FEATS, OWN, hid_part, BLK),
            shape(first_rows, width, dtype=F32),
        ),
        in_specs=[VMEM] * 7,
        out_specs=(ANY, VMEM, VMEM),
        scratch_shapes=[
            buf(FEATS, OWN, feat_part, BLK),
            buf(OWN, width, BLK),
            buf(NB, hid_part, BLK),
            buf(NB, hid_part, BLK),
            buf(FEATS, OWN, hid_part, BLK),
            buf(FEATS, first_rows, width, dtype=F32),
            buf(FEATS, first_rows, width, dtype=F32),
            buf(SIDE, first_rows, width, dtype=F32),
            buf(SIDE, first_rows, width, dtype=F32),
            middle_bufs,
            dma(2, 5, 4),
            dma(2, 5, 4),
            dma(2, 2, 2, 3),
            dma(2, 2, 2, 3),
            dma(3, FEATS - 1),
            dma(3, FEATS - 1),
            dma(FEATS - 1 + 2 * (SIDE - 1)),
            dma(FEATS - 1 + 2 * (SIDE - 1)),
            pltpu.SemaphoreType.DMA,
        ],
        compiler_params=remote(2),
        name="first_layer",
    )(
        feat_mean,
        back_parts.reshape(SIDE, SIDE, NB, hid_part, BLK),
        own_feats,
        all_weights1,
        bias1.reshape(width, 1),
        all_weights2,
        cotangent,
    )

    hidden_mean = pl.pallas_call(
        mean_kernel,
        out_shape=shape(NB, hid_part, BLK),
        in_specs=[SMEM, SMEM, ANY, VMEM, VMEM],
        out_specs=VMEM,
        scratch_shapes=[held, buf(NB, hid_part, BLK, dtype=F32), listed, dma(STAGES, BATCH)],
        compiler_params=plain,
        name="aggregate_hidden",
    )(tile_cols, tile_counts, groups, all_hidden.reshape(block_total, hid_part, BLK), degree_rows)

    second_rows = 2 * hid_part
    hidden_out, grad_second = pl.pallas_call(
        functools.partial(last_kernel, scale),
        out_shape=(shape(own_nodes, width), shape(second_rows, width, dtype=F32)),
        in_specs=[VMEM] * 5,
        out_specs=(VMEM, VMEM),
        scratch_shapes=[
            buf(FEATS, OWN, hid_part, BLK),
            buf(FEATS, second_rows, width, dtype=F32),
            buf(FEATS, second_rows, width, dtype=F32),
            buf(SIDE, second_rows, width, dtype=F32),
            buf(SIDE, second_rows, width, dtype=F32),
            dma(FEATS - 1),
            dma(FEATS - 1),
            dma(FEATS - 1 + 2 * (SIDE - 1)),
            dma(FEATS - 1 + 2 * (SIDE - 1)),
        ],
        compiler_params=remote(3),
        name="second_layer",
    )(hidden_mean, hidden, all_weights2, bias2.reshape(1, width), cotangent)
    return (
        hidden_out,
        grad_second.reshape(2, hid_part, width),
        grad_first.reshape(2, feat_part, width),
    )


def solution(mesh):
    return jax.shard_map(
        shards,
        mesh=mesh,
        in_specs=(
            P("feat", "node"),
            P("node", None),
            P("node"),
            P("node", None, None, None),
            P("node"),
            P(None, "feat", None),
            P(),
            P(None, "feat", None),
            P(),
            P(("node", "feat"), None),
        ),
        out_specs=(P(("node", "feat"), None), P(None, "feat", None), P(None, "feat", None)),
        check_vma=False,
    )
```

time: 627 us -> 187 us (0.30)
  waiting for transfers between devices: 404 us -> 0 us
  Pallas kernels: 0 us -> 171 us
  blocking collectives: 85.9 us -> 0 us
  matrix products: 79.8 us -> 0 us
  between operations: 14.3 us -> 0.74 us
  local copies, waits for them, and re-layouts: 26.6 us -> 13.5 us
  other arithmetic: 10.2 us -> 0 us
    pallas_call x0 -> x5, Pallas kernels: none -> 171 us  [the longest x1 80 us: shards(): pl.pallas_call(functools.partial(middle_kernel, scale), out_shape=(shape(...]
    psum x1 -> x0, waiting for transfers between devices: 160 us -> none  [shards(): second_total = lax.psum(second_partial, 'node')]
    all_gather x4 -> x0, waiting for transfers between devices: 151 us -> none  [the longest x1 60.5 us: shards(): all_hidden = lax.all_gather(hidden_cols, 'node', axis=1, tiled=True)]
    reduce_scatter x2 -> x0, waiting for transfers between devices: 83 us -> none  [the longest x1 42.3 us: shards(): lax.psum_scatter(lax.dot_general(picked_cols, second_weights, (((0,), (0,...]
    dot_general x9 -> x0, matrix products: 79.8 us -> none  [the longest x1 29.1 us: shards(): lax.dot_general(selector, contrib, (((0,), (0,)), ((), ())), precision=la...]
    psum x1 -> x0, blocking collectives: 74.5 us -> none  [shards(): first_total = lax.psum(first_partial, 'node')]
    gather x2 -> x0, local copies, waits for them, and re-layouts: 11.5 us -> none  [aggregate(): picked = jnp.take(blocks, tile_cols, axis=1)]
    all_to_all x1 -> x0, blocking collectives: 11.4 us -> none  [shards(): lax.all_to_all(hidden.T, 'feat', split_axis=0, concat_axis=1, tiled=True)]
  transfers between devices with their start and end apart: 8 -> 0, of which waited for: 8 -> 0; matrix products, arithmetic and copies ran while one was open for 3% -> 0% of each run, Pallas kernels for 0% -> 0%
where the time goes in v1:
time: 187 us; the launch traced here: 185 us
  Pallas kernels  171 us (91%)
  local copies, waits for them, and re-layouts  13.5 us (7%)
    pallas_call x1, Pallas kernels, shards(): pl.pallas_call(functools.partial(middle_kernel, scale), out_shape=(shape(...  80 us
    pallas_call x1, Pallas kernels, shards(): pl.pallas_call(gather_kernel, out_shape=(shape(shard_total, NB, feat_part...  28.7 us
    pallas_call x1, Pallas kernels, shards(): pl.pallas_call(functools.partial(last_kernel, scale), out_shape=(shape(ow...  26.9 us
    pallas_call x1, Pallas kernels, shards(): pl.pallas_call(both_kernel, out_shape=(shape(NB, feat_part, BLK), shape(b...  20.2 us
    pallas_call x1, Pallas kernels, shards(): pl.pallas_call(mean_kernel, out_shape=shape(NB, hid_part, BLK), in_specs=...  15.3 us
    unnamed x28, local copies, waits for them, and re-layouts  12.7 us

profile of v1, /device:TPU:0, one launch (start us, length us, event | category | flops | bytes accessed | tf_op | source)
XLA Modules:
  0.0 185.5 jit_solution(7703853437441885526)
XLA Ops:
  0.6 0.8 copy.17.cols
  1.4 0.8 copy.16.bias1
  2.2 0.0 copy-start.1
  2.2 1.0 copy-done.1
  3.2 0.0 copy-start.4
  3.2 0.7 copy-done.4
  4.0 0.0 copy-start.6
  4.0 0.9 copy-done.6
  4.9 0.0 copy-start.7
  4.9 0.8 copy-done.7
  5.6 0.0 copy-start.8
  5.6 0.7 copy-done.8
  6.4 28.7 %gather_features.1 = (bf16[16,48,16,128]{3,2,1,0:T(8,128)(2,1)S(1)}, bf16[8,6,16,128]{3,2,1,0:T(8,128)(2,1)S(1)}, bf16[8,2,16,256]{3,2,1,0:T(8,128)(2,1)S(1)}, b...) custom-call(bf16[16,6144]{1,0:T(8,128)(2,1)S(1)} %copy-done.6, bf16[2,16,256]{2,1,0:T(8,128)(2,1)S(1)} %copy-done.8, ...), custom_call_target="tpu_custom_call" | custom-call | tf_op jit(solution)/shard_map/gather_features/pallas_call | solution.py:599
  35.1 0.0 copy-start.3
  35.1 1.7 copy-done.3
  36.8 0.0 copy-start.5
  36.8 0.7 copy-done.5
  37.6 0.0 copy-start.9
  37.6 0.7 copy-done.9
  38.2 0.0 copy-start.2
  38.2 20.2 %aggregate_both.1 = (bf16[48,16,128]{2,1,0:T(8,128)(2,1)S(1)}, bf16[768,32,128]{2,1,0:T(8,128)(2,1)}) custom-call(s32[48,16]{1,0:T(8,128)S(1)} %copy.17.cols, s32[48]{0:T(128)S(1)} %copy-done.9, bf16[192,4,128,128]{3,2,1,0:T(8,128)(2,1)} %bitcast.19, bf16[768,16,128]{2,1,0:T(8,128)(2,1)} %bitcast.11, bf16[48,32,128]{2,1,0:T(8,128)(2,1)S(1)} %bitcast.12, ...), custom_call_target="tpu_custom_call" | custom-call | tf_op jit(solution)/shard_map/aggregate_both/pallas_call | solution.py:626
  58.4 0.0 copy-start.10
  58.5 0.0 copy-done.2
  58.5 80.0 %first_layer.1 = (bf16[16,48,32,128]{3,2,1,0:T(8,128)(2,1)S(1)}, bf16[8,6,32,128]{3,2,1,0:T(8,128)(2,1)S(1)}, f32[32,256]{1,0:T(8,128)S(1)}) custom-call(bf16[48,16,128]{2,1,0:T(8,128)(2,1)S(1)} %get-tuple-element.17.feat_mean, bf16[4,4,48,32,128]{4,3,2,1,0:T(8,128)(2,1)} %bitcast.21, bf16[8,6,16,128]{3,2,1,0:T(8,128)(2,1)S(1)} %get-tuple-element.19.own_feats, ...), custom_call_target="tpu_custom_call" | custom-call | tf_op jit(solution)/shard_map/first_layer/pallas_call | solution.py:661
  138.5 0.0 copy-start
  138.5 2.6 %copy-done = bf16[16,48,32,128]{3,2,1,0:T(8,128)(2,1)} copy-done((bf16[16,48,32,128]{3,2,1,0:T(8,128)(2,1)}, bf16[16,48,32,128]{3,2,1,0:T(8,128)(2,1)S(1)}, u32[]{:S(2)}) %copy-start) | copy-done | bytes 6291480
  141.2 0.0 copy-done.10
  141.2 0.0 copy-start.11
  141.2 15.3 %aggregate_hidden.1.hidden_mean = bf16[48,32,128]{2,1,0:T(8,128)(2,1)S(1)} custom-call(s32[48,16]{1,0:T(8,128)S(1)} %copy.17.cols, s32[48]{0:T(128)S(1)} %copy-done.10, bf16[192,4,128,128]{3,2,1,0:T(8,128)(2,1)} %bitcast.20, bf16[768,32,128]{2,1,0:T(8,128)(2,1)} %bitcast.10, s32[48,128]{1,0:T(8,128)S(1)} %bitcast.15), custom_call_target="tpu_custom_call" | custom-call | tf_op jit(solution)/shard_map/aggregate_hidden/pallas_call | solution.py:703
  156.5 0.0 copy-done.11
  156.5 26.9 %second_layer.1 = (bf16[768,256]{1,0:T(8,128)(2,1)S(1)}, f32[64,256]{1,0:T(8,128)S(1)}) custom-call(bf16[48,32,128]{2,1,0:T(8,128)(2,1)S(1)} %aggregate_hidden.1.hidden_mean, bf16[8,6,32,128]{3,2,1,0:T(8,128)(2,1)S(1)} %get-tuple-element.23.hidden, bf16[8,2,32,256]{3,2,1,0:T(8,128)(2,1)S(1)} %get-tuple-element.21.weights2, f32[1,256]{1,0:T(1,128)S(1)} %bitcast.18, ...), custom_call_target="tpu_custom_call" | custom-call | tf_op jit(solution)/shard_map/second_layer/pallas_call | solution.py:714
  183.5 0.7 copy.21
  184.2 0.6 copy.22
  184.8 0.6 copy.23
Async XLA Ops:
  2.2 1.0 copy-start.1
  3.2 0.7 copy-start.4
  4.0 0.9 copy-start.6
  4.9 0.8 copy-start.7
  5.6 0.7 copy-start.8
  35.1 1.7 copy-start.3
  36.8 0.7 copy-start.5
  37.6 0.7 copy-start.9
  38.2 20.2 %copy-start.2 = (bf16[768,256]{1,0:T(8,128)(2,1)S(1)}, bf16[768,256]{1,0:T(8,128)(2,1)}, u32[]{:S(2)}) copy-start(bf16[768,256]{1,0:T(8,128)(2,1)} %cotangent.5) | copy-start | bytes 1179652
  58.4 82.7 %copy-start.10 = (s32[48]{0:T(128)S(1)}, s32[48]{0:T(128)}, u32[]{:S(2)}) copy-start(s32[48]{0:T(128)} %counts.3) | copy-start | bytes 580
  138.5 2.7 %copy-start = (bf16[16,48,32,128]{3,2,1,0:T(8,128)(2,1)}, bf16[16,48,32,128]{3,2,1,0:T(8,128)(2,1)S(1)}, u32[]{:S(2)}) copy-start(bf16[16,48,32,128]{3,2,1,0:T(8,128)(2,1)S(1)} %get-tuple-element.22) | copy-start | bytes 18874372
  141.2 15.3 %copy-start.11 = (f32[256]{0:T(256)S(1)}, f32[256]{0:T(256)}, u32[]{:S(2)}) copy-start(f32[256]{0:T(256)} %param.18) | copy-start | bytes 3076

commit v2 on v1

--- a/solution.py
+++ b/solution.py
@@ -18,12 +18,13 @@
 OWN = NB // FEATS
 HALF, QUARTER = NB // 2, NB // 4
 GROUP = 4
-BATCH = 4
+BATCH = 8
 STAGES = 4
 AHEAD = (0, -1, 1, 2)
 VMEM = pl.BlockSpec(memory_space=pltpu.VMEM)
 SMEM = pl.BlockSpec(memory_space=pltpu.SMEM)
 ANY = pl.BlockSpec(memory_space=pl.ANY)
+HBM = pl.BlockSpec(memory_space=pltpu.HBM)
 
 
 def dot(left, right, dims):
@@ -43,15 +44,20 @@
     def shift(self, dx, dz):
         return ((self.x + dx + SIDE) % SIDE) * SIDE + (self.z + dz + SIDE) % SIDE
 
+    def beside(self):
+        return [self.shift(dx, dz) for dx, dz in ((1, 0), (-1, 0), (0, 1), (0, -1))]
+
+    def others(self):
+        total = SIDE * SIDE
+        return [(self.node + step) % total for step in range(1, total)]
+
     def turned(self, half, first, second):
         return self.shift(first, second) if half == 0 else self.shift(second, first)
 
-    def greet(self, far):
+    def greet(self, nodes):
         barrier = pltpu.get_barrier_semaphore()
-        steps = (1, 2, 3) if far else (1, 3)
         others = [{"feat": self.peer(step)} for step in range(1, FEATS)]
-        others += [{"node": self.shift(step, 0)} for step in steps]
-        others += [{"node": self.shift(0, step)} for step in steps]
+        others += [{"node": node} for node in nodes]
         for other in others:
             pl.semaphore_signal(barrier, inc=1, device_id=other, device_id_type=MESH)
         pl.semaphore_wait(barrier, len(others))
@@ -80,8 +86,7 @@
 
 
 class Regroup:
-    def __init__(self, copies, place, source_at, target_at, send_sems, recv_sems):
-        self.place, self.source_at, self.target_at = place, source_at, target_at
+    def __init__(self, copies, place, source_at, target_at, send_sems, recv_sems, own=True):
         self.parts = []
         for step in range(1, FEATS):
             to = place.peer(step)
@@ -94,7 +99,8 @@
                     {"feat": to},
                 )
             )
-        target_at(place.feat)[...] = source_at(place.feat)[...]
+        if own:
+            target_at(place.feat)[...] = source_at(place.feat)[...]
 
     def wait(self):
         for part in self.parts:
@@ -161,8 +167,8 @@
             self.arrived(half, SIDE)
             self.full(half, 3)
 
-    def far(self):
-        for unit in range(1, SIDE):
+    def far(self, units=(1, 2, 3)):
+        for unit in units:
             for role in range(2):
                 for half in range(2):
                     self.forward(half, unit, role)
@@ -267,49 +273,37 @@
 
 
 class Total:
-    def __init__(self, copies, place, part, feat_buf, x_buf, z_buf, send_sems, recv_sems):
-        self.copies, self.place, self.part = copies, place, part
-        self.bufs = (feat_buf, x_buf, z_buf)
-        self.sems = (send_sems, recv_sems)
-
-    def over_feat(self):
-        buf = self.bufs[0]
-        sends, recvs = self.sems
-        self.regroup = Regroup(
-            self.copies,
-            self.place,
-            lambda to: self.part.at[to],
-            lambda slot: buf.at[slot],
-            sends.at[pl.ds(0, FEATS - 1)],
-            recvs.at[pl.ds(0, FEATS - 1)],
-        )
-
-    def _spread(self, axis, value):
-        buf, place = self.bufs[1 + axis], self.place
-        sends, recvs = self.sems
-        at = place.x if axis == 0 else place.z
-        buf[at] = value
+    def __init__(self, copies, place, part, came, summed, send_sems, recv_sems):
+        self.copies, self.place, self.part, self.came, self.summed = copies, place, part, came, summed
+        self.send_sems, self.recv_sems = send_sems, recv_sems
+
+    def _all(self, phase, source_at, target):
+        place = self.place
         self.parts = []
-        for step in range(1, SIDE):
-            slot = FEATS - 1 + axis * (SIDE - 1) + step - 1
-            to = place.shift(step, 0) if axis == 0 else place.shift(0, step)
+        for number, node in enumerate(place.others()):
             self.parts.append(
-                self.copies.send(buf.at[at], buf.at[at], sends.at[slot], recvs.at[slot], {"node": to})
+                self.copies.send(
+                    source_at(node),
+                    target.at[place.node],
+                    self.send_sems.at[phase, number],
+                    self.recv_sems.at[phase, number],
+                    {"node": node},
+                )
             )
 
-    def over_x(self):
-        self.regroup.wait()
-        self._spread(0, sum(self.bufs[0][slot] for slot in range(FEATS)))
-
-    def over_z(self):
+    def start(self):
+        self._all(0, lambda node: self.part.at[node], self.came)
+        self.came[self.place.node] = self.part[self.place.node]
+
+    def turn(self):
         for part in self.parts:
             part.wait_recv()
-        self._spread(1, sum(self.bufs[1][slot] for slot in range(SIDE)))
+        self.summed[self.place.node] = sum(self.came[slot] for slot in range(SIDE * SIDE))
+        self._all(1, lambda node: self.summed.at[self.place.node], self.summed)
 
     def end(self):
         for part in self.parts:
             part.wait_recv()
-        return sum(self.bufs[2][slot] for slot in range(SIDE))
 
 
 def own_rows(feat):
@@ -317,30 +311,41 @@
 
 
 def gather_kernel(
-    features, weights1, weights2, cotangent, degrees,
+    features_in, weights1, weights2, cotangent_in, degrees_in,
     all_feats, own_feats, all_weights1, all_weights2, spread,
-    blocks, outgoing, gather_send, gather_recv, feat_send, feat_recv, local_sem,
+    features, cotangent, degrees, own_weights1, own_weights2, blocks, outgoing,
+    gather_send, gather_recv, feat_send, feat_recv, local_sems,
 ):
     place, copies = Place(), Copies()
-    place.greet(False)
-    regroups = [
-        Regroup(
-            copies, place, lambda to: weights, lambda slot: target.at[slot], feat_send.at[number], feat_recv.at[number]
-        )
-        for number, (weights, target) in enumerate(((weights2, all_weights2), (weights1, all_weights1)))
-    ]
+    pairs = (
+        (features_in, features),
+        (weights2, own_weights2),
+        (weights1, own_weights1),
+        (cotangent_in, cotangent),
+        (degrees_in, degrees),
+    )
+    loads = [pltpu.make_async_copy(pair[0], pair[1], local_sems.at[number]) for number, pair in enumerate(pairs)]
+    for load in loads:
+        load.start()
+    place.greet(place.beside())
+    loads[0].wait()
     for block in range(NB):
         blocks[block] = features[:, block * BLK : (block + 1) * BLK]
     gather = Gather(copies, place, blocks, all_feats, gather_send, gather_recv)
     gather.start()
-    own = pltpu.make_async_copy(blocks, all_feats.at[place.node], local_sem)
+    regroups = []
+    for number, (weights, target) in enumerate(((own_weights2, all_weights2), (own_weights1, all_weights1))):
+        loads[1 + number].wait()
+        regroups.append(
+            Regroup(
+                copies, place, lambda to: weights, lambda slot: target.at[slot], feat_send.at[number], feat_recv.at[number]
+            )
+        )
+    own = pltpu.make_async_copy(blocks, all_feats.at[place.node], local_sems.at[len(pairs)])
     own.start()
-    regroups.append(
-        Regroup(
-            copies, place, lambda to: blocks.at[own_rows(to)], lambda slot: own_feats.at[slot], feat_send.at[2], feat_recv.at[2]
-        )
-    )
     gather.rows()
+    loads[3].wait()
+    loads[4].wait()
     regroups[0].wait()
     neighbour = all_weights2[:, 1].reshape(-1, all_weights2.shape[-1])
     for block in range(OWN):
@@ -354,6 +359,11 @@
         )
     )
     gather.near()
+    regroups.append(
+        Regroup(
+            copies, place, lambda to: blocks.at[own_rows(to)], lambda slot: own_feats.at[slot], feat_send.at[2], feat_recv.at[2]
+        )
+    )
     gather.far()
     for regroup in regroups[1:]:
         regroup.wait()
@@ -412,7 +422,7 @@
     block, first, live, wide = entry
     parts = []
     for slot in range(GROUP):
-        value = source[cols[block, first + slot]]
+        value = source[cols[first + slot, block]]
         parts.append(jnp.where(first + slot < live, value, jnp.zeros_like(value)))
     return dot(jnp.concatenate(parts, axis=1), wide, ((1,), (1,)))
 
@@ -439,7 +449,7 @@
         for (block, first, live, _), product in zip(entries, backs):
             for slot in range(GROUP):
                 part = product[:, slot * BLK : (slot + 1) * BLK]
-                back_sums[cols[block, first + slot]] += jnp.where(first + slot < live, part, jnp.zeros_like(part))
+                back_sums[cols[first + slot, block]] += jnp.where(first + slot < live, part, jnp.zeros_like(part))
 
     each_step(counts, groups, tiles, held, tile_sems, work)
     write_mean(sums, degrees, mean)
@@ -450,7 +460,9 @@
         back[rows] = back_sums[rows].astype(BF16)
 
 
-def mean_kernel(cols, counts, tiles, source, degrees, mean, held, sums, groups, tile_sems):
+def mean_kernel(
+    cols, counts, tiles, source, degrees, hidden, cotangent, mean, grads, held, sums, groups, tile_sems
+):
     sums[...] = jnp.zeros_like(sums)
 
     def work(entries):
@@ -460,23 +472,42 @@
 
     each_step(counts, groups, tiles, held, tile_sems, work)
     write_mean(sums, degrees, mean)
+    wide = 8
+    total = jnp.zeros((2 * hidden.shape[1], cotangent.shape[-1]), F32)
+
+    def add(part, total):
+        blocks = [part * wide + block for block in range(wide)]
+        stack = [jnp.concatenate([hidden[block], mean[block]], axis=0) for block in blocks]
+        nodes = cotangent[pl.ds(part * wide, wide)].reshape(wide * BLK, -1)
+        return total + dot(jnp.concatenate(stack, axis=1), nodes, ((1,), (0,)))
+
+    put_tiles(grads, lax.fori_loop(0, NB // wide, add, total))
+
+
+def put_tiles(out, value):
+    for tile in range(out.shape[0]):
+        out[tile] = value[tile // 2 * 8 : tile // 2 * 8 + 8, tile % 2 * BLK : tile % 2 * BLK + BLK]
 
 
 def middle_kernel(
-    scale, feat_mean, back_parts, own_feats, weights1, bias1, weights2, cotangent,
-    all_hidden, hidden, grad_first,
-    means, slopes, own_hidden, back, own_back, grads, feat_buf, x_buf, z_buf, bufs,
-    gather_send, gather_recv, scatter_send, scatter_recv, feat_send, feat_recv, total_send, total_recv, local_sem,
+    feat_mean, back_parts, own_feats, weights1, bias1, weights2, cotangent_in,
+    all_hidden, hidden, own_hidden, all_cotangent, grad_first,
+    cotangent, means, slopes, back, own_back, grads, feat_buf, bufs,
+    gather_send, gather_recv, scatter_send, scatter_recv, feat_send, feat_recv, local_sems,
 ):
     place, copies = Place(), Copies()
-    place.greet(True)
-    to_means = Regroup(
-        copies, place, lambda to: feat_mean.at[own_rows(to)], lambda slot: means.at[slot], feat_send.at[0], feat_recv.at[0]
-    )
+    load = pltpu.make_async_copy(cotangent_in, cotangent, local_sems.at[0])
+    load.start()
+    place.greet(place.beside())
+
+    def regroup(number, source_at, target_at, own=True):
+        return Regroup(copies, place, source_at, target_at, feat_send.at[number], feat_recv.at[number], own)
+
+    to_means = regroup(0, lambda to: feat_mean.at[own_rows(to)], lambda slot: means.at[slot])
     scatter = Scatter(copies, place, back_parts, bufs, scatter_send, scatter_recv)
     scatter.start()
-    width = weights1.shape[-1]
-    first = weights1[...].reshape(-1, width)
+    first = weights1[...].reshape(-1, weights1.shape[-1])
+    bias = jnp.transpose(jnp.broadcast_to(bias1[...], (BLK, bias1.shape[1])))
     to_means.wait()
 
     def stack(block):
@@ -486,27 +517,28 @@
         return jnp.concatenate(parts, axis=0)
 
     for block in range(OWN):
-        pre = dot(first, stack(block), ((0,), (0,))) + bias1[...]
+        pre = dot(first, stack(block), ((0,), (0,))) + bias
         sigmoid = jax.nn.sigmoid(pre)
         slopes[block] = (sigmoid * (1.0 + pre * (1.0 - sigmoid))).astype(BF16)
         hidden[:, block] = (pre * sigmoid).astype(BF16).reshape(FEATS, -1, BLK)
-    to_hidden = Regroup(
-        copies, place, lambda to: hidden.at[to], lambda slot: own_hidden.at[own_rows(slot)], feat_send.at[1], feat_recv.at[1]
-    )
+    to_hidden = regroup(1, lambda to: hidden.at[to], lambda slot: own_hidden.at[own_rows(slot)])
     scatter.middle()
     to_hidden.wait()
     gather = Gather(copies, place, own_hidden, all_hidden, gather_send, gather_recv)
-    own = pltpu.make_async_copy(own_hidden, all_hidden.at[place.node], local_sem)
+    gather.start()
+    own = pltpu.make_async_copy(own_hidden, all_hidden.at[place.node], local_sems.at[1])
     own.start()
+    load.wait()
+    to_cotangent = regroup(4, lambda to: cotangent, lambda slot: all_cotangent.at[slot], False)
+    own_cotangent = pltpu.make_async_copy(cotangent, all_cotangent.at[place.feat], local_sems.at[2])
+    own_cotangent.start()
     scatter.turn()
-    gather.start()
+    gather.rows()
     scatter.middle2()
-    gather.rows()
+    gather.near()
     scatter.end(back)
-    to_back = Regroup(
-        copies, place, lambda to: back.at[own_rows(to)], lambda slot: own_back.at[slot], feat_send.at[2], feat_recv.at[2]
-    )
-    gather.near()
+    to_back = regroup(2, lambda to: back.at[own_rows(to)], lambda slot: own_back.at[slot])
+    gather.far((1,))
     to_back.wait()
     own_weights = weights2[:, 0].reshape(-1, weights2.shape[-1])
     total = None
@@ -518,56 +550,57 @@
         product = dot(stack(block), grad, ((1,), (1,)))
         total = product if total is None else total + product
     grads[...] = total.reshape(grads.shape)
-    summed = Total(copies, place, grads, feat_buf, x_buf, z_buf, total_send, total_recv)
-    summed.over_feat()
-    gather.far()
-    summed.over_x()
-    summed.over_z()
-    grad_first[...] = summed.end() * scale
+    to_total = regroup(3, lambda to: grads.at[to], lambda slot: feat_buf.at[slot])
+    gather.far((2, 3))
+    to_total.wait()
+    put_tiles(grad_first, sum(feat_buf[slot] for slot in range(FEATS)))
     gather.last()
+    to_cotangent.wait()
+    own_cotangent.wait()
     own.wait()
     copies.finish()
 
 
 def last_kernel(
-    scale, hidden_mean, hidden, weights2, bias2, cotangent,
-    hidden_out, grad_second,
-    means, grads, feat_buf, x_buf, z_buf, feat_send, feat_recv, total_send, total_recv,
+    hidden_mean, grad_first, grad_second,
+    means, summed,
+    part, came, feat_send, feat_recv, total_send, total_recv,
 ):
     place, copies = Place(), Copies()
-    place.greet(True)
+    place.greet(place.others())
     to_means = Regroup(
         copies, place, lambda to: hidden_mean.at[own_rows(to)], lambda slot: means.at[slot], feat_send, feat_recv
     )
+    part[:, 1] = jnp.zeros_like(part[:, 1])
+    part[:, 0] = grad_second[...]
+    part[pl.ds(0, grad_first.shape[0]), 1] = grad_first[...]
+    total = Total(copies, place, part, came, summed, total_send, total_recv)
+    total.start()
+    total.turn()
+    total.end()
+    to_means.wait()
+    copies.finish()
+
+
+def out_kernel(scale, hidden, means, weights2, bias2, summed, hidden_out, grad_second, grad_first):
     second = weights2[...].reshape(-1, weights2.shape[-1])
-    to_means.wait()
-
-    def stack(block):
+    for block in range(OWN):
         parts = []
         for part in range(FEATS):
             parts += [hidden[part, block], means[part, block]]
-        return jnp.concatenate(parts, axis=0)
-
-    total = None
-    for block in range(OWN):
-        nodes = cotangent[block * BLK : (block + 1) * BLK, :]
-        product = dot(stack(block), nodes, ((1,), (0,)))
-        total = product if total is None else total + product
-    grads[...] = total.reshape(grads.shape)
-    summed = Total(copies, place, grads, feat_buf, x_buf, z_buf, total_send, total_recv)
-    summed.over_feat()
-    for block in range(OWN):
-        out = dot(stack(block), second, ((0,), (0,))) + bias2[...]
+        out = dot(jnp.concatenate(parts, axis=0), second, ((0,), (0,))) + bias2[...]
         hidden_out[block * BLK : (block + 1) * BLK, :] = out.astype(BF16)
-    summed.over_x()
-    summed.over_z()
-    grad_second[...] = summed.end() * scale
-    copies.finish()
-
-
-def remote(collective_id):
+    for kind, grad in enumerate((grad_second, grad_first)):
+        for tile in range(grad.shape[0] // 8 * 2):
+            rows, columns = pl.ds(tile // 2 * 8, 8), pl.ds(tile % 2 * BLK, BLK)
+            grad[rows, columns] = summed[tile, kind] * scale
+
+
+def limit(mib, collective_id=None):
+    if collective_id is None:
+        return pltpu.CompilerParams(vmem_limit_bytes=mib * 1024 * 1024)
     return pltpu.CompilerParams(
-        collective_id=collective_id, has_side_effects=True, vmem_limit_bytes=44 * 1024 * 1024
+        collective_id=collective_id, has_side_effects=True, vmem_limit_bytes=mib * 1024 * 1024
     )
 
 
@@ -605,24 +638,29 @@
             shape(FEATS, 2, hid_part, width),
             shape(FEATS, OWN, hid_part, BLK),
         ),
-        in_specs=[VMEM] * 5,
+        in_specs=[HBM] * 5,
         out_specs=(ANY, VMEM, VMEM, VMEM, VMEM),
         scratch_shapes=[
+            buf(*features.shape),
+            buf(own_nodes, width),
+            buf(NB, BLK, dtype=jnp.int32),
+            buf(*weights1.shape),
+            buf(*weights2.shape),
             buf(NB, feat_part, BLK),
             buf(FEATS, OWN, hid_part, BLK),
             dma(2, 5, 4),
             dma(2, 5, 4),
             dma(4, FEATS - 1),
             dma(4, FEATS - 1),
-            pltpu.SemaphoreType.DMA,
+            dma(6),
         ],
-        compiler_params=remote(1),
+        compiler_params=limit(12, 1),
         name="gather_features",
     )(features, weights1, weights2, cotangent, degree_rows)
 
     held = buf(STAGES, BATCH, GROUP, BLK, BLK)
     listed = pltpu.SMEM((NB * 4 + 2 * BATCH,), jnp.int32)
-    plain = pltpu.CompilerParams(vmem_limit_bytes=52 * 1024 * 1024)
+    slot_cols = tile_cols.T
     feat_mean, back_parts = pl.pallas_call(
         both_kernel,
         out_shape=(shape(NB, feat_part, BLK), shape(block_total, hid_part, BLK)),
@@ -635,10 +673,10 @@
             listed,
             dma(STAGES, BATCH),
         ],
-        compiler_params=plain,
+        compiler_params=limit(36),
         name="aggregate_both",
     )(
-        tile_cols,
+        slot_cols,
         tile_counts,
         groups,
         all_feats.reshape(block_total, feat_part, BLK),
@@ -657,79 +695,94 @@
         buf(2, 2, *row[1:]),
         buf(2, 2, *part_row[1:]),
     )
-    first_rows = 2 * feat_part
-    all_hidden, hidden, grad_first = pl.pallas_call(
-        functools.partial(middle_kernel, scale),
+    first_rows, second_rows = 2 * feat_part, 2 * hid_part
+    all_hidden, hidden, own_hidden, all_cotangent, first_part = pl.pallas_call(
+        middle_kernel,
         out_shape=(
             shape(shard_total, NB, hid_part, BLK),
             shape(FEATS, OWN, hid_part, BLK),
-            shape(first_rows, width, dtype=F32),
+            shape(NB, hid_part, BLK),
+            shape(FEATS, own_nodes, width),
+            shape(first_rows // 8 * 2, 8, BLK, dtype=F32),
         ),
-        in_specs=[VMEM] * 7,
-        out_specs=(ANY, VMEM, VMEM),
+        in_specs=[VMEM] * 6 + [HBM],
+        out_specs=(ANY, VMEM, VMEM, ANY, VMEM),
         scratch_shapes=[
+            buf(own_nodes, width),
             buf(FEATS, OWN, feat_part, BLK),
             buf(OWN, width, BLK),
-            buf(NB, hid_part, BLK),
             buf(NB, hid_part, BLK),
             buf(FEATS, OWN, hid_part, BLK),
             buf(FEATS, first_rows, width, dtype=F32),
             buf(FEATS, first_rows, width, dtype=F32),
-            buf(SIDE, first_rows, width, dtype=F32),
-            buf(SIDE, first_rows, width, dtype=F32),
             middle_bufs,
             dma(2, 5, 4),
             dma(2, 5, 4),
             dma(2, 2, 2, 3),
             dma(2, 2, 2, 3),
-            dma(3, FEATS - 1),
-            dma(3, FEATS - 1),
-            dma(FEATS - 1 + 2 * (SIDE - 1)),
-            dma(FEATS - 1 + 2 * (SIDE - 1)),
-            pltpu.SemaphoreType.DMA,
+            dma(5, FEATS - 1),
+            dma(5, FEATS - 1),
+            dma(3),
         ],
-        compiler_params=remote(2),
+        compiler_params=limit(24, 2),
         name="first_layer",
     )(
         feat_mean,
         back_parts.reshape(SIDE, SIDE, NB, hid_part, BLK),
         own_feats,
         all_weights1,
-        bias1.reshape(width, 1),
+        bias1.reshape(1, width),
         all_weights2,
         cotangent,
     )
 
-    hidden_mean = pl.pallas_call(
+    hidden_mean, second_part = pl.pallas_call(
         mean_kernel,
-        out_shape=shape(NB, hid_part, BLK),
-        in_specs=[SMEM, SMEM, ANY, VMEM, VMEM],
-        out_specs=VMEM,
+        out_shape=(shape(NB, hid_part, BLK), shape(second_rows // 8 * 2, 8, BLK, dtype=F32)),
+        in_specs=[SMEM, SMEM, ANY, VMEM, VMEM, VMEM, VMEM],
+        out_specs=(VMEM, VMEM),
         scratch_shapes=[held, buf(NB, hid_part, BLK, dtype=F32), listed, dma(STAGES, BATCH)],
-        compiler_params=plain,
+        compiler_params=limit(24),
         name="aggregate_hidden",
-    )(tile_cols, tile_counts, groups, all_hidden.reshape(block_total, hid_part, BLK), degree_rows)
-
-    second_rows = 2 * hid_part
-    hidden_out, grad_second = pl.pallas_call(
-        functools.partial(last_kernel, scale),
-        out_shape=(shape(own_nodes, width), shape(second_rows, width, dtype=F32)),
-        in_specs=[VMEM] * 5,
+    )(
+        slot_cols,
+        tile_counts,
+        groups,
+        all_hidden.reshape(block_total, hid_part, BLK),
+        degree_rows,
+        own_hidden,
+        all_cotangent.reshape(NB, BLK, width),
+    )
+
+    pieces = (shard_total, 2, 8, BLK)
+    means, summed = pl.pallas_call(
+        last_kernel,
+        out_shape=(shape(FEATS, OWN, hid_part, BLK), shape(*pieces, dtype=F32)),
+        in_specs=[VMEM] * 3,
         out_specs=(VMEM, VMEM),
         scratch_shapes=[
-            buf(FEATS, OWN, hid_part, BLK),
-            buf(FEATS, second_rows, width, dtype=F32),
-            buf(FEATS, second_rows, width, dtype=F32),
-            buf(SIDE, second_rows, width, dtype=F32),
-            buf(SIDE, second_rows, width, dtype=F32),
+            buf(*pieces, dtype=F32),
+            buf(*pieces, dtype=F32),
             dma(FEATS - 1),
             dma(FEATS - 1),
-            dma(FEATS - 1 + 2 * (SIDE - 1)),
-            dma(FEATS - 1 + 2 * (SIDE - 1)),
+            dma(2, shard_total - 1),
+            dma(2, shard_total - 1),
         ],
-        compiler_params=remote(3),
+        compiler_params=limit(8, 3),
+        name="regroup_mean",
+    )(hidden_mean, first_part, second_part)
+    hidden_out, grad_second, grad_first = pl.pallas_call(
+        functools.partial(out_kernel, scale),
+        out_shape=(
+            shape(own_nodes, width),
+            shape(second_rows, width, dtype=F32),
+            shape(first_rows, width, dtype=F32),
+        ),
+        in_specs=[VMEM] * 5,
+        out_specs=(VMEM, VMEM, VMEM),
+        compiler_params=limit(8),
         name="second_layer",
-    )(hidden_mean, hidden, all_weights2, bias2.reshape(1, width), cotangent)
+    )(hidden, means, all_weights2, bias2.reshape(1, width), summed)
     return (
         hidden_out,
         grad_second.reshape(2, hid_part, width),

time: 187 us -> 155 us (0.83)
  Pallas kernels: 171 us -> 148 us
  local copies, waits for them, and re-layouts: 13.5 us -> 6.24 us
    pallas_call x3 -> x4, Pallas kernels: 122 us -> 109 us  [the longest x1 77.3 us: shards(): pl.pallas_call(middle_kernel, out_shape=(shape(shard_total, NB, hid_part,...]
    pallas_call x1, Pallas kernels: 20.2 us -> 9.16 us  [shards(): pl.pallas_call(both_kernel, out_shape=(shape(NB, feat_part, BLK), shape(b...]
    unnamed x28 -> x26, local copies, waits for them, and re-layouts: 12.7 us -> 6.24 us
where the time goes in v2:
time: 155 us
  Pallas kernels  148 us (95%)
  local copies, waits for them, and re-layouts  6.24 us (4%)
    pallas_call x1, Pallas kernels, shards(): pl.pallas_call(middle_kernel, out_shape=(shape(shard_total, NB, hid_part,...  77.3 us
    pallas_call x1, Pallas kernels, shards(): pl.pallas_call(gather_kernel, out_shape=(shape(shard_total, NB, feat_part...  29.3 us
    pallas_call x1, Pallas kernels, shards(): pl.pallas_call(last_kernel, out_shape=(shape(FEATS, OWN, hid_part, BLK),...  22.7 us
    pallas_call x1, Pallas kernels, shards(): pl.pallas_call(both_kernel, out_shape=(shape(NB, feat_part, BLK), shape(b...  9.16 us
    pallas_call x1, Pallas kernels, shards(): pl.pallas_call(mean_kernel, out_shape=(shape(NB, hid_part, BLK), shape(se...  8.04 us
    unnamed x26, local copies, waits for them, and re-layouts  6.24 us

profile of v2, /device:TPU:0, one launch (start us, length us, event | category | flops | bytes accessed | tf_op | source)
XLA Modules:
  0.0 154.7 jit_solution(11136233173160998003)
XLA Ops:
  0.6 0.0 copy-start
  0.6 1.0 copy-done
  1.6 0.0 copy-start.2
  1.6 0.7 copy-done.2
  2.4 0.0 copy-start.4
  2.4 0.9 copy-done.4
  3.3 0.0 copy-start.5
  3.3 0.8 copy-done.5
  4.1 0.0 copy-start.8
  4.1 0.7 copy-done.8
  4.8 29.3 %gather_features.1 = (bf16[16,48,16,128]{3,2,1,0:T(8,128)(2,1)S(1)}, bf16[8,6,16,128]{3,2,1,0:T(8,128)(2,1)S(1)}, bf16[8,2,16,256]{3,2,1,0:T(8,128)(2,1)S(1)}, b...) custom-call(bf16[16,6144]{1,0:T(8,128)(2,1)S(1)} %copy-done.4, bf16[2,16,256]{2,1,0:T(8,128)(2,1)S(1)} %copy-done.8, ...), custom_call_target="tpu_custom_call" | custom-call | tf_op jit(solution)/shard_map/gather_features/pallas_call | solution.py:632
  34.1 0.0 copy-start.3
  34.1 0.7 copy-done.3
  34.9 0.0 copy-start.6
  34.9 0.7 copy-done.6
  35.6 0.0 copy-start.9
  35.6 0.7 copy-done.9
  36.2 0.0 copy-start.1
  36.2 0.0 copy-start.12
  36.2 9.2 %aggregate_both.1 = (bf16[48,16,128]{2,1,0:T(8,128)(2,1)S(1)}, bf16[768,32,128]{2,1,0:T(8,128)(2,1)S(1)}) custom-call(s32[16,48]{1,0:T(8,128)S(1)} %bitcast.20, s32[48]{0:T(128)S(1)} %copy-done.9, bf16[192,4,128,128]{3,2,1,0:T(8,128)(2,1)} %bitcast.24, bf16[768,16,128]{2,1,0:T(8,128)(2,1)S(1)} %bitcast.14, bf16[48,32,128]{2,1,0:T(8,128)(2,1)S(1)} %bitcast.16, ...), custom_call_target="tpu_custom_call" | custom-call | tf_op jit(solution)/shard_map/aggregate_both/pallas_call | solution.py:664
  45.4 0.0 copy-start.7
  45.4 0.0 copy-start.10
  45.4 0.0 copy-done.1
  45.4 0.0 copy-done.12
  45.4 77.3 %first_layer.1 = (bf16[16,48,32,128]{3,2,1,0:T(8,128)(2,1)S(1)}, bf16[8,6,32,128]{3,2,1,0:T(8,128)(2,1)S(1)}, bf16[48,32,128]{2,1,0:T(8,128)(2,1)S(1)}, bf16[8,768,256]{2,1,0:T(8,128)(2,1)S(1)}, f32[8,8,128]{2,1,0:T(8,128)S(1)}) custom-call(bf16[48,16,128]{2,1,0:T(8,128)(2,1)S(1)} %get-tuple-element.24.feat_mean, bf16[4,4,48,32,128]{4,3,2,1,0:T(8,128)(2,1)S(1)} %bitcast.12, ...), custom_call_target="tpu_custom_call" | custom-call | tf_op jit(solution)/shard_map/first_layer/pallas_call | solution.py:699
  122.7 0.0 copy-done.7
  122.7 0.0 copy-done.10
  122.7 0.0 copy-start.11
  122.8 8.0 %aggregate_hidden.1 = (bf16[48,32,128]{2,1,0:T(8,128)(2,1)S(1)}, f32[16,8,128]{2,1,0:T(8,128)S(1)}) custom-call(s32[16,48]{1,0:T(8,128)S(1)} %bitcast.21, s32[48]{0:T(128)S(1)} %copy-done.10, bf16[192,4,128,128]{3,2,1,0:T(8,128)(2,1)} %bitcast.25, bf16[768,32,128]{2,1,0:T(8,128)(2,1)S(1)} %bitcast.13, s32[48,128]{1,0:T(8,128)S(1)} %bitcast.19, ...), custom_call_target="tpu_custom_call" | custom-call | tf_op jit(solution)/shard_map/aggregate_hidden/pallas_call | solution.py:739
  130.8 22.7 %regroup_mean.1 = (bf16[8,6,32,128]{3,2,1,0:T(8,128)(2,1)S(1)}, f32[16,2,8,128]{3,2,1,0:T(8,128)S(1)}) custom-call(bf16[48,32,128]{2,1,0:T(8,128)(2,1)S(1)} %get-tuple-element.33.hidden_mean, f32[8,8,128]{2,1,0:T(8,128)S(1)} %get-tuple-element.34.grad_first, f32[16,8,128]{2,1,0:T(8,128)S(1)} %get-tuple-element.35.grad_second), custom_call_target="tpu_custom_call" | custom-call | tf_op jit(solution)/shard_map/regroup_mean/pallas_call | solution.py:758
  153.5 0.0 copy-done.11
  153.5 1.2 second_layer.1
Async XLA Ops:
  0.6 1.0 copy-start
  1.6 0.7 copy-start.2
  2.4 0.9 copy-start.4
  3.3 0.8 copy-start.5
  4.1 0.7 copy-start.8
  34.1 0.7 copy-start.3
  34.9 0.7 copy-start.6
  35.6 0.7 copy-start.9
  36.2 9.2 %copy-start.1 = (bf16[768,256]{1,0:T(8,128)(2,1)S(1)}, bf16[768,256]{1,0:T(8,128)(2,1)}, u32[]{:S(2)}) copy-start(bf16[768,256]{1,0:T(8,128)(2,1)} %cotangent_in.3) | copy-start | bytes 1179652
  36.2 9.2 %copy-start.12 = (f32[256]{0:T(256)S(1)}, f32[256]{0:T(256)}, u32[]{:S(2)}) copy-start(f32[256]{0:T(256)} %param.16) | copy-start | bytes 3076
  45.4 77.3 %copy-start.7 = (s32[48,16]{0,1:T(8,128)S(1)}, s32[48,16]{0,1:T(8,128)}, u32[]{:S(2)}) copy-start(s32[48,16]{0,1:T(8,128)} %param.11) | copy-start | bytes 9220
  45.4 77.3 %copy-start.10 = (s32[48]{0:T(128)S(1)}, s32[48]{0:T(128)}, u32[]{:S(2)}) copy-start(s32[48]{0:T(128)} %counts.3) | copy-start | bytes 580
  122.7 30.7 %copy-start.11 = (f32[256]{0:T(256)S(1)}, f32[256]{0:T(256)}, u32[]{:S(2)}) copy-start(f32[256]{0:T(256)} %param.18) | copy-start | bytes 3076

commit v3 on v2

--- a/solution.py
+++ b/solution.py
@@ -20,6 +20,7 @@
 GROUP = 4
 BATCH = 8
 STAGES = 4
+ROW_STAGES = 3
 AHEAD = (0, -1, 1, 2)
 VMEM = pl.BlockSpec(memory_space=pltpu.VMEM)
 SMEM = pl.BlockSpec(memory_space=pltpu.SMEM)
@@ -39,7 +40,7 @@
         self.z = self.node % SIDE
 
     def peer(self, step):
-        return (self.feat + step) % FEATS
+        return (self.feat + step + FEATS) % FEATS
 
     def shift(self, dx, dz):
         return ((self.x + dx + SIDE) % SIDE) * SIDE + (self.z + dz + SIDE) % SIDE
@@ -86,7 +87,7 @@
 
 
 class Regroup:
-    def __init__(self, copies, place, source_at, target_at, send_sems, recv_sems, own=True):
+    def __init__(self, copies, place, source_at, target_at, send_sems, recv_sems):
         self.parts = []
         for step in range(1, FEATS):
             to = place.peer(step)
@@ -99,11 +100,35 @@
                     {"feat": to},
                 )
             )
-        if own:
-            target_at(place.feat)[...] = source_at(place.feat)[...]
+        target_at(place.feat)[...] = source_at(place.feat)[...]
 
     def wait(self):
         for part in self.parts:
+            part.wait_recv()
+
+
+class Broadcast:
+    def __init__(self, copies, place, source, target, send_sems, recv_sems):
+        self.copies, self.place, self.target = copies, place, target
+        self.send_sems, self.recv_sems = send_sems, recv_sems
+        self.other = place.feat + 1 - 2 * (place.feat % 2)
+        slot = target.at[place.feat]
+        self.parts = [self._send(step - 1, source, slot, place.peer(2 * step)) for step in range(1, SIDE)]
+        self.parts.append(self._send(SIDE - 1, source, slot, self.other))
+
+    def _send(self, number, source, target, to):
+        return self.copies.send(
+            source, target, self.send_sems.at[number], self.recv_sems.at[number], {"feat": to}
+        )
+
+    def forward(self):
+        for step in range(1, SIDE):
+            self.parts[step - 1].wait_recv()
+            slot = self.target.at[self.place.peer(-2 * step)]
+            self.parts.append(self._send(SIDE - 1 + step, slot, slot, self.other))
+
+    def wait(self):
+        for part in self.parts[SIDE - 1 :]:
             part.wait_recv()
 
 
@@ -150,6 +175,8 @@
     def start(self):
         for half in range(2):
             self.full(half, SIDE)
+
+    def start_columns(self):
         for half in range(2):
             self.full(half, 0)
 
@@ -214,6 +241,8 @@
         for half in range(2):
             for side, way in ((0, 1), (1, -1)):
                 self._send(half, 0, side, 0, self._line(half, 2 * way, side), self.pass1.at[half, side])
+
+    def direct(self):
         for half in range(2):
             for side, way in ((0, 1), (1, -1)):
                 rows = pl.ds((1 - side) * QUARTER, QUARTER)
@@ -333,6 +362,7 @@
         blocks[block] = features[:, block * BLK : (block + 1) * BLK]
     gather = Gather(copies, place, blocks, all_feats, gather_send, gather_recv)
     gather.start()
+    gather.start_columns()
     regroups = []
     for number, (weights, target) in enumerate(((own_weights2, all_weights2), (own_weights1, all_weights1))):
         loads[1 + number].wait()
@@ -384,33 +414,32 @@
     return total
 
 
-def each_step(counts, groups, tiles, held, tile_sems, work):
+def each_step(counts, groups, tiles, held, tile_sems, clear, work):
     total = plan_groups(counts, groups)
     steps = (total + BATCH - 1) // BATCH
-
-    def copy(step, place):
-        slot = step % STAGES
-        group = groups[step * BATCH + place]
-        return pltpu.make_async_copy(tiles.at[group], held.at[slot, place], tile_sems.at[slot, place])
 
     def fetch(step):
         @pl.when(step < steps)
         def _():
+            slot = step % STAGES
             for place in range(BATCH):
-                copy(step, place).start()
+                group = groups[step * BATCH + place]
+                pltpu.make_async_copy(tiles.at[group], held.at[slot, place], tile_sems.at[slot]).start()
 
     for step in range(STAGES - 1):
         fetch(step)
+    clear()
 
     def body(step, carry):
         fetch(step + STAGES - 1)
+        slot = step % STAGES
+        pltpu.make_async_copy(tiles.at[pl.ds(0, BATCH)], held.at[slot], tile_sems.at[slot]).wait()
         entries = []
         for place in range(BATCH):
-            copy(step, place).wait()
             group = groups[step * BATCH + place]
             block, first = group // 4, (group % 4) * GROUP
             live = jnp.where(step * BATCH + place < total, counts[block], 0)
-            wide = jnp.concatenate([held[step % STAGES, place, slot] for slot in range(GROUP)], axis=1)
+            wide = jnp.concatenate([held[slot, place, part] for part in range(GROUP)], axis=1)
             entries.append((block, first, live, wide))
         work(entries)
         return carry
@@ -427,51 +456,58 @@
     return dot(jnp.concatenate(parts, axis=1), wide, ((1,), (1,)))
 
 
-def write_mean(sums, degrees, mean):
-    @pl.loop(0, NB)
-    def _(block):
-        mean[block] = (sums[block] / degrees[pl.ds(block, 1), :].astype(F32)).astype(BF16)
-
-
-def both_kernel(cols, counts, tiles, source, spread, degrees, mean, back, held, sums, back_sums, groups, tile_sems):
-    sums[...] = jnp.zeros_like(sums)
-
-    @pl.loop(0, back_sums.shape[0] // 16)
-    def _(part):
-        rows = pl.ds(part * 16, 16)
-        back_sums[rows] = jnp.zeros((16,) + back_sums.shape[1:], F32)
+def load_all(pairs, sems):
+    loads = [pltpu.make_async_copy(pair[0], pair[1], sems.at[number]) for number, pair in enumerate(pairs)]
+    for load in loads:
+        load.start()
+    for load in loads:
+        load.wait()
+
+
+def back_kernel(cols_in, counts_in, tiles, spread, back, cols, counts, held, sums, groups, tile_sems, load_sems):
+    load_all(((cols_in, cols), (counts_in, counts)), load_sems)
+
+    def clear():
+        @pl.loop(0, sums.shape[0] // 16)
+        def _(part):
+            sums[pl.ds(part * 16, 16)] = jnp.zeros((16,) + sums.shape[1:], F32)
 
     def work(entries):
-        products = [picked(source, cols, entry) for entry in entries]
         backs = [dot(spread[entry[0]], entry[3], ((1,), (0,))) for entry in entries]
-        for entry, product in zip(entries, products):
-            sums[entry[0]] += product
         for (block, first, live, _), product in zip(entries, backs):
             for slot in range(GROUP):
                 part = product[:, slot * BLK : (slot + 1) * BLK]
-                back_sums[cols[first + slot, block]] += jnp.where(first + slot < live, part, jnp.zeros_like(part))
-
-    each_step(counts, groups, tiles, held, tile_sems, work)
-    write_mean(sums, degrees, mean)
-
-    @pl.loop(0, back_sums.shape[0] // 16)
+                sums[cols[first + slot, block]] += jnp.where(first + slot < live, part, jnp.zeros_like(part))
+
+    each_step(counts, groups, tiles, held, tile_sems, clear, work)
+
+    @pl.loop(0, sums.shape[0] // 16)
     def _(part):
         rows = pl.ds(part * 16, 16)
-        back[rows] = back_sums[rows].astype(BF16)
+        back[rows] = sums[rows].astype(BF16)
 
 
 def mean_kernel(
-    cols, counts, tiles, source, degrees, hidden, cotangent, mean, grads, held, sums, groups, tile_sems
+    cols_in, counts_in, tiles, source, degrees_in, hidden, cotangent,
+    mean, grads,
+    cols, counts, degrees, held, sums, groups, tile_sems, load_sems,
 ):
-    sums[...] = jnp.zeros_like(sums)
+    load_all(((cols_in, cols), (counts_in, counts), (degrees_in, degrees)), load_sems)
+
+    def clear():
+        sums[...] = jnp.zeros_like(sums)
 
     def work(entries):
         products = [picked(source, cols, entry) for entry in entries]
         for entry, product in zip(entries, products):
             sums[entry[0]] += product
 
-    each_step(counts, groups, tiles, held, tile_sems, work)
-    write_mean(sums, degrees, mean)
+    each_step(counts, groups, tiles, held, tile_sems, clear, work)
+
+    @pl.loop(0, NB)
+    def _(block):
+        mean[block] = (sums[block] / degrees[pl.ds(block, 1), :].astype(F32)).astype(BF16)
+
     wide = 8
     total = jnp.zeros((2 * hidden.shape[1], cotangent.shape[-1]), F32)
 
@@ -490,25 +526,69 @@
 
 
 def middle_kernel(
-    feat_mean, back_parts, own_feats, weights1, bias1, weights2, cotangent_in,
+    cols, counts, tiles, all_feats, degrees, back_parts, own_feats, weights1, bias1, weights2, cotangent_in,
     all_hidden, hidden, own_hidden, all_cotangent, grad_first,
-    cotangent, means, slopes, back, own_back, grads, feat_buf, bufs,
-    gather_send, gather_recv, scatter_send, scatter_recv, feat_send, feat_recv, local_sems,
+    held, cotangent, feat_mean, means, slopes, back, own_back, grads, feat_buf, bufs,
+    gather_send, gather_recv, scatter_send, scatter_recv, feat_send, feat_recv, tile_sems, local_sems,
 ):
     place, copies = Place(), Copies()
+
+    def tile_copy(step):
+        slot = step % ROW_STAGES
+        return pltpu.make_async_copy(tiles.at[own_rows(place.peer(step + 1))], held.at[slot], tile_sems.at[slot])
+
+    for step in range(ROW_STAGES - 1):
+        tile_copy(step).start()
     load = pltpu.make_async_copy(cotangent_in, cotangent, local_sems.at[0])
     load.start()
     place.greet(place.beside())
 
-    def regroup(number, source_at, target_at, own=True):
-        return Regroup(copies, place, source_at, target_at, feat_send.at[number], feat_recv.at[number], own)
-
-    to_means = regroup(0, lambda to: feat_mean.at[own_rows(to)], lambda slot: means.at[slot])
+    def regroup(number, source_at, target_at):
+        return Regroup(copies, place, source_at, target_at, feat_send.at[number], feat_recv.at[number])
+
+    def mean_copy(step):
+        to = place.peer(step + 1)
+        return pltpu.make_async_remote_copy(
+            src_ref=feat_mean.at[own_rows(to)],
+            dst_ref=means.at[place.feat],
+            send_sem=feat_send.at[0, step],
+            recv_sem=feat_recv.at[0, step],
+            device_id={"feat": to},
+            device_id_type=MESH,
+        )
+
+    def own_blocks(step):
+        tile_copy(step).wait()
+        for part in range(OWN):
+            block = place.peer(step + 1) * OWN + part
+            parts = []
+            for slot in range(tiles.shape[1]):
+                value = all_feats[cols[slot, block]]
+                parts.append(jnp.where(slot < counts[block], value, jnp.zeros_like(value)))
+            wide = jnp.concatenate([held[step % ROW_STAGES, part, slot] for slot in range(tiles.shape[1])], axis=1)
+            total = dot(jnp.concatenate(parts, axis=1), wide, ((1,), (1,)))
+            feat_mean[block] = (total / degrees[pl.ds(block, 1), :].astype(F32)).astype(BF16)
+
+    def send_blocks(step, carry):
+        @pl.when(step + ROW_STAGES - 1 < FEATS)
+        def _():
+            tile_copy(step + ROW_STAGES - 1).start()
+
+        own_blocks(step)
+        mean_copy(step).start()
+        return carry
+
     scatter = Scatter(copies, place, back_parts, bufs, scatter_send, scatter_recv)
     scatter.start()
     first = weights1[...].reshape(-1, weights1.shape[-1])
     bias = jnp.transpose(jnp.broadcast_to(bias1[...], (BLK, bias1.shape[1])))
-    to_means.wait()
+    lax.fori_loop(0, 3, send_blocks, jnp.int32(0))
+    scatter.direct()
+    lax.fori_loop(3, FEATS - 1, send_blocks, jnp.int32(0))
+    own_blocks(FEATS - 1)
+    means[place.feat] = feat_mean[own_rows(place.feat)]
+    for step in range(FEATS - 1):
+        mean_copy(step).wait()
 
     def stack(block):
         parts = []
@@ -529,16 +609,17 @@
     own = pltpu.make_async_copy(own_hidden, all_hidden.at[place.node], local_sems.at[1])
     own.start()
     load.wait()
-    to_cotangent = regroup(4, lambda to: cotangent, lambda slot: all_cotangent.at[slot], False)
+    to_cotangent = Broadcast(copies, place, cotangent, all_cotangent, feat_send.at[4], feat_recv.at[4])
     own_cotangent = pltpu.make_async_copy(cotangent, all_cotangent.at[place.feat], local_sems.at[2])
     own_cotangent.start()
     scatter.turn()
+    gather.start_columns()
     gather.rows()
     scatter.middle2()
     gather.near()
     scatter.end(back)
     to_back = regroup(2, lambda to: back.at[own_rows(to)], lambda slot: own_back.at[slot])
-    gather.far((1,))
+    gather.far((1, 2))
     to_back.wait()
     own_weights = weights2[:, 0].reshape(-1, weights2.shape[-1])
     total = None
@@ -551,7 +632,8 @@
         total = product if total is None else total + product
     grads[...] = total.reshape(grads.shape)
     to_total = regroup(3, lambda to: grads.at[to], lambda slot: feat_buf.at[slot])
-    gather.far((2, 3))
+    gather.far((3,))
+    to_cotangent.forward()
     to_total.wait()
     put_tiles(grad_first, sum(feat_buf[slot] for slot in range(FEATS)))
     gather.last()
@@ -614,6 +696,10 @@
 
 def dma(*dims):
     return pltpu.SemaphoreType.DMA(dims)
+
+
+def in_hbm(array):
+    return pltpu.with_memory_space_constraint(array, pltpu.HBM)
 
 
 def shards(
@@ -656,33 +742,28 @@
         ],
         compiler_params=limit(12, 1),
         name="gather_features",
-    )(features, weights1, weights2, cotangent, degree_rows)
+    )(*[in_hbm(array) for array in (features, weights1, weights2, cotangent, degree_rows)])
 
     held = buf(STAGES, BATCH, GROUP, BLK, BLK)
-    listed = pltpu.SMEM((NB * 4 + 2 * BATCH,), jnp.int32)
+    planned = pltpu.SMEM((NB * 4 + 2 * BATCH,), jnp.int32)
     slot_cols = tile_cols.T
-    feat_mean, back_parts = pl.pallas_call(
-        both_kernel,
-        out_shape=(shape(NB, feat_part, BLK), shape(block_total, hid_part, BLK)),
-        in_specs=[SMEM, SMEM, ANY, VMEM, VMEM, VMEM],
-        out_specs=(VMEM, VMEM),
+    listed = [pltpu.SMEM((tiles.shape[1], NB), jnp.int32), pltpu.SMEM((NB,), jnp.int32)]
+    back_parts = pl.pallas_call(
+        back_kernel,
+        out_shape=shape(block_total, hid_part, BLK),
+        in_specs=[HBM, HBM, ANY, VMEM],
+        out_specs=VMEM,
         scratch_shapes=[
+            *listed,
             held,
-            buf(NB, feat_part, BLK, dtype=F32),
             buf(block_total, hid_part, BLK, dtype=F32),
-            listed,
-            dma(STAGES, BATCH),
+            planned,
+            dma(STAGES),
+            dma(2),
         ],
-        compiler_params=limit(36),
-        name="aggregate_both",
-    )(
-        slot_cols,
-        tile_counts,
-        groups,
-        all_feats.reshape(block_total, feat_part, BLK),
-        spread.reshape(NB, hid_part, BLK),
-        degree_rows,
-    )
+        compiler_params=limit(28),
+        name="aggregate_back",
+    )(in_hbm(slot_cols), in_hbm(tile_counts), groups, spread.reshape(NB, hid_part, BLK))
 
     row = (SIDE, HALF, hid_part, BLK)
     part_row = (SIDE, QUARTER, hid_part, BLK)
@@ -705,10 +786,12 @@
             shape(FEATS, own_nodes, width),
             shape(first_rows // 8 * 2, 8, BLK, dtype=F32),
         ),
-        in_specs=[VMEM] * 6 + [HBM],
+        in_specs=[SMEM, SMEM, ANY] + [VMEM] * 7 + [HBM],
         out_specs=(ANY, VMEM, VMEM, ANY, VMEM),
         scratch_shapes=[
+            buf(ROW_STAGES, OWN, *tiles.shape[1:]),
             buf(own_nodes, width),
+            buf(NB, feat_part, BLK),
             buf(FEATS, OWN, feat_part, BLK),
             buf(OWN, width, BLK),
             buf(NB, hid_part, BLK),
@@ -722,34 +805,47 @@
             dma(2, 2, 2, 3),
             dma(5, FEATS - 1),
             dma(5, FEATS - 1),
+            dma(ROW_STAGES),
             dma(3),
         ],
-        compiler_params=limit(24, 2),
+        compiler_params=limit(32, 2),
         name="first_layer",
     )(
-        feat_mean,
+        slot_cols,
+        tile_counts,
+        tiles,
+        all_feats.reshape(block_total, feat_part, BLK),
+        degree_rows,
         back_parts.reshape(SIDE, SIDE, NB, hid_part, BLK),
         own_feats,
         all_weights1,
         bias1.reshape(1, width),
         all_weights2,
-        cotangent,
+        in_hbm(cotangent),
     )
 
     hidden_mean, second_part = pl.pallas_call(
         mean_kernel,
         out_shape=(shape(NB, hid_part, BLK), shape(second_rows // 8 * 2, 8, BLK, dtype=F32)),
-        in_specs=[SMEM, SMEM, ANY, VMEM, VMEM, VMEM, VMEM],
+        in_specs=[HBM, HBM, ANY, VMEM, HBM, VMEM, VMEM],
         out_specs=(VMEM, VMEM),
-        scratch_shapes=[held, buf(NB, hid_part, BLK, dtype=F32), listed, dma(STAGES, BATCH)],
+        scratch_shapes=[
+            *listed,
+            buf(NB, BLK, dtype=jnp.int32),
+            held,
+            buf(NB, hid_part, BLK, dtype=F32),
+            planned,
+            dma(STAGES),
+            dma(3),
+        ],
         compiler_params=limit(24),
         name="aggregate_hidden",
     )(
-        slot_cols,
-        tile_counts,
+        in_hbm(slot_cols),
+        in_hbm(tile_counts),
         groups,
         all_hidden.reshape(block_total, hid_part, BLK),
-        degree_rows,
+        in_hbm(degree_rows),
         own_hidden,
         all_cotangent.reshape(NB, BLK, width),
     )

time: 155 us -> 136 us (0.88)
  Pallas kernels: 148 us -> 135 us
  local copies, waits for them, and re-layouts: 6.24 us -> 0.03 us
    unnamed x26 -> x10, local copies, waits for them, and re-layouts: 6.24 us -> 0.03 us
    pallas_call x1, Pallas kernels: 77.3 us -> 72.4 us  [shards(): pl.pallas_call(middle_kernel, out_shape=(shape(shard_total, NB, hid_part,...]
    pallas_call x1, Pallas kernels: 22.7 us -> 19 us  [shards(): pl.pallas_call(last_kernel, out_shape=(shape(FEATS, OWN, hid_part, BLK),...]
    pallas_call x1, Pallas kernels: 9.16 us -> 6.09 us  [shards(): pl.pallas_call(back_kernel, out_shape=shape(block_total, hid_part, BLK),...]
where the time goes in v3:
time: 136 us
  Pallas kernels  135 us (99%)
    pallas_call x1, Pallas kernels, shards(): pl.pallas_call(middle_kernel, out_shape=(shape(shard_total, NB, hid_part,...  72.4 us
    pallas_call x1, Pallas kernels, shards(): pl.pallas_call(gather_kernel, out_shape=(shape(shard_total, NB, feat_part...  28.9 us
    pallas_call x1, Pallas kernels, shards(): pl.pallas_call(last_kernel, out_shape=(shape(FEATS, OWN, hid_part, BLK),...  19 us
    pallas_call x1, Pallas kernels, shards(): pl.pallas_call(mean_kernel, out_shape=(shape(NB, hid_part, BLK), shape(se...  7.46 us
    pallas_call x1, Pallas kernels, shards(): pl.pallas_call(back_kernel, out_shape=shape(block_total, hid_part, BLK),...  6.09 us

profile of v3, /device:TPU:0, one launch (start us, length us, event | category | flops | bytes accessed | tf_op | source)
XLA Modules:
  0.0 135.8 jit_solution(1784694093920344071)
XLA Ops:
  0.6 28.9 %gather_features.1 = (bf16[16,48,16,128]{3,2,1,0:T(8,128)(2,1)S(1)}, bf16[8,6,16,128]{3,2,1,0:T(8,128)(2,1)S(1)}, bf16[8,2,16,256]{3,2,1,0:T(8,128)(2,1)S(1)}, b...) custom-call(bf16[16,6144]{1,0:T(8,128)(2,1)} %features_in.1, bf16[2,16,256]{2,1,0:T(8,128)(2,1)} %weights1.1, ...), custom_call_target="tpu_custom_call" | custom-call | tf_op jit(solution)/shard_map/gather_features/pallas_call | solution.py:718
  29.6 0.0 copy-start
  29.6 0.0 copy-start.1
  29.6 0.0 copy-start.2
  29.6 0.0 copy-start.3
  29.6 6.1 %aggregate_back.1 = bf16[768,32,128]{2,1,0:T(8,128)(2,1)S(1)} custom-call(s32[16,48]{1,0:T(8,128)} %bitcast.20, s32[48]{0:T(128)} %counts_in.3, bf16[192,4,128,128]{3,2,1,0:T(8,128)(2,1)} %bitcast.25, bf16[48,32,128]{2,1,0:T(8,128)(2,1)S(1)} %bitcast.16), custom_call_target="tpu_custom_call" | custom-call | tf_op jit(solution)/shard_map/aggregate_back/pallas_call | solution.py:751
  35.7 0.0 copy-done
  35.7 0.0 copy-done.1
  35.7 0.0 copy-done.2
  35.7 0.0 copy-done.3
  35.8 72.4 %first_layer.1 = (bf16[16,48,32,128]{3,2,1,0:T(8,128)(2,1)S(1)}, bf16[8,6,32,128]{3,2,1,0:T(8,128)(2,1)S(1)}, bf16[48,32,128]{2,1,0:T(8,128)(2,1)S(1)}, bf16[8,768,256]{2,1,0:T(8,128)(2,1)S(1)}, f32[8,8,128]{2,1,0:T(8,128)S(1)}) custom-call(s32[16,48]{1,0:T(8,128)S(1)} %bitcast.22, s32[48]{0:T(128)S(1)} %copy-done.2, bf16[48,16,128,128]{3,2,1,0:T(8,128)(2,1)} %tiles.1, ...), custom_call_target="tpu_custom_call" | custom-call | tf_op jit(solution)/shard_map/first_layer/pallas_call | solution.py:780
  108.2 0.0 copy-start.4
  108.2 7.5 %aggregate_hidden.1 = (bf16[48,32,128]{2,1,0:T(8,128)(2,1)S(1)}, f32[16,8,128]{2,1,0:T(8,128)S(1)}) custom-call(s32[16,48]{1,0:T(8,128)} %bitcast.21, s32[48]{0:T(128)} %counts_in.3, bf16[192,4,128,128]{3,2,1,0:T(8,128)(2,1)} %bitcast.26, bf16[768,32,128]{2,1,0:T(8,128)(2,1)S(1)} %bitcast.13, s32[48,128]{1,0:T(8,128)} %bitcast.18, ...), custom_call_target="tpu_custom_call" | custom-call | tf_op jit(solution)/shard_map/aggregate_hidden/pallas_call | solution.py:827
  115.7 19.0 %regroup_mean.1 = (bf16[8,6,32,128]{3,2,1,0:T(8,128)(2,1)S(1)}, f32[16,2,8,128]{3,2,1,0:T(8,128)S(1)}) custom-call(bf16[48,32,128]{2,1,0:T(8,128)(2,1)S(1)} %get-tuple-element.29.hidden_mean, f32[8,8,128]{2,1,0:T(8,128)S(1)} %get-tuple-element.30.grad_first, f32[16,8,128]{2,1,0:T(8,128)S(1)} %get-tuple-element.31.grad_second), custom_call_target="tpu_custom_call" | custom-call | tf_op jit(solution)/shard_map/regroup_mean/pallas_call | solution.py:854
  134.7 0.0 copy-done.4
  134.7 1.2 second_layer.1
Async XLA Ops:
  29.6 6.2 %copy-start = (s32[6144]{0:T(1024)S(1)}, s32[6144]{0:T(1024)}, u32[]{:S(2)}) copy-start(s32[6144]{0:T(1024)} %param.14) | copy-start | bytes 73732
  29.6 6.1 %copy-start.1 = (s32[48,16]{0,1:T(8,128)S(1)}, s32[48,16]{0,1:T(8,128)}, u32[]{:S(2)}) copy-start(s32[48,16]{0,1:T(8,128)} %param.11) | copy-start | bytes 9220
  29.6 6.1 %copy-start.2 = (s32[48]{0:T(128)S(1)}, s32[48]{0:T(128)}, u32[]{:S(2)}) copy-start(s32[48]{0:T(128)} %counts_in.3) | copy-start | bytes 580
  29.6 6.1 %copy-start.3 = (f32[256]{0:T(256)S(1)}, f32[256]{0:T(256)}, u32[]{:S(2)}) copy-start(f32[256]{0:T(256)} %param.16) | copy-start | bytes 3076
  108.2 26.5 %copy-start.4 = (f32[256]{0:T(256)S(1)}, f32[256]{0:T(256)}, u32[]{:S(2)}) copy-start(f32[256]{0:T(256)} %param.18) | copy-start | bytes 3076

commit v4 on v3

--- a/solution.py
+++ b/solution.py
@@ -107,31 +107,6 @@
             part.wait_recv()
 
 
-class Broadcast:
-    def __init__(self, copies, place, source, target, send_sems, recv_sems):
-        self.copies, self.place, self.target = copies, place, target
-        self.send_sems, self.recv_sems = send_sems, recv_sems
-        self.other = place.feat + 1 - 2 * (place.feat % 2)
-        slot = target.at[place.feat]
-        self.parts = [self._send(step - 1, source, slot, place.peer(2 * step)) for step in range(1, SIDE)]
-        self.parts.append(self._send(SIDE - 1, source, slot, self.other))
-
-    def _send(self, number, source, target, to):
-        return self.copies.send(
-            source, target, self.send_sems.at[number], self.recv_sems.at[number], {"feat": to}
-        )
-
-    def forward(self):
-        for step in range(1, SIDE):
-            self.parts[step - 1].wait_recv()
-            slot = self.target.at[self.place.peer(-2 * step)]
-            self.parts.append(self._send(SIDE - 1 + step, slot, slot, self.other))
-
-    def wait(self):
-        for part in self.parts[SIDE - 1 :]:
-            part.wait_recv()
-
-
 class Gather:
     def __init__(self, copies, place, own, out, send_sems, recv_sems):
         self.copies, self.place, self.own, self.out = copies, place, own, out
@@ -261,11 +236,14 @@
                 rows = pl.ds(side * QUARTER, QUARTER)
                 self._send(half, 0, side, 2, total, self.got1.at[half, side, :, rows])
 
-    def turn(self):
+    def lines_arrived(self):
         for half in range(2):
             for side in range(2):
                 for kind in (1, 2):
                     self.made[half, 0, side, kind].wait_recv()
+
+    def turn(self):
+        for half in range(2):
             mine, left, right, total = self._line(half, 0), self.got1.at[half, 0], self.got1.at[half, 1], self.half1.at[half]
 
             @pl.loop(0, SIDE)
@@ -301,36 +279,17 @@
                 out[pl.ds(half * HALF + quarter * QUARTER, QUARTER)] = total.astype(BF16)
 
 
-class Total:
-    def __init__(self, copies, place, part, came, summed, send_sems, recv_sems):
-        self.copies, self.place, self.part, self.came, self.summed = copies, place, part, came, summed
-        self.send_sems, self.recv_sems = send_sems, recv_sems
-
-    def _all(self, phase, source_at, target):
-        place = self.place
+class Exchange:
+    def __init__(self, copies, place, source_at, target, send_sems, recv_sems):
         self.parts = []
         for number, node in enumerate(place.others()):
             self.parts.append(
-                self.copies.send(
-                    source_at(node),
-                    target.at[place.node],
-                    self.send_sems.at[phase, number],
-                    self.recv_sems.at[phase, number],
-                    {"node": node},
+                copies.send(
+                    source_at(node), target.at[place.node], send_sems.at[number], recv_sems.at[number], {"node": node}
                 )
             )
 
-    def start(self):
-        self._all(0, lambda node: self.part.at[node], self.came)
-        self.came[self.place.node] = self.part[self.place.node]
-
-    def turn(self):
-        for part in self.parts:
-            part.wait_recv()
-        self.summed[self.place.node] = sum(self.came[slot] for slot in range(SIDE * SIDE))
-        self._all(1, lambda node: self.summed.at[self.place.node], self.summed)
-
-    def end(self):
+    def wait(self):
         for part in self.parts:
             part.wait_recv()
 
@@ -363,7 +322,17 @@
     gather = Gather(copies, place, blocks, all_feats, gather_send, gather_recv)
     gather.start()
     gather.start_columns()
-    regroups = []
+    loads[3].wait()
+    loads[4].wait()
+    for block in range(OWN):
+        nodes = jnp.transpose(cotangent[block * BLK : (block + 1) * BLK, :].astype(F32))
+        degree = degrees[pl.ds(place.feat * OWN + block, 1), :].astype(F32)
+        outgoing[:, block] = (nodes / degree).astype(BF16).reshape(FEATS, -1, BLK)
+    regroups = [
+        Regroup(
+            copies, place, lambda to: outgoing.at[to], lambda slot: spread.at[slot], feat_send.at[3], feat_recv.at[3]
+        )
+    ]
     for number, (weights, target) in enumerate(((own_weights2, all_weights2), (own_weights1, all_weights1))):
         loads[1 + number].wait()
         regroups.append(
@@ -374,20 +343,6 @@
     own = pltpu.make_async_copy(blocks, all_feats.at[place.node], local_sems.at[len(pairs)])
     own.start()
     gather.rows()
-    loads[3].wait()
-    loads[4].wait()
-    regroups[0].wait()
-    neighbour = all_weights2[:, 1].reshape(-1, all_weights2.shape[-1])
-    for block in range(OWN):
-        nodes = cotangent[block * BLK : (block + 1) * BLK, :]
-        back = dot(neighbour, nodes, ((1,), (1,)))
-        degree = degrees[pl.ds(place.feat * OWN + block, 1), :].astype(F32)
-        outgoing[:, block] = (back / degree).astype(BF16).reshape(FEATS, -1, BLK)
-    regroups.append(
-        Regroup(
-            copies, place, lambda to: outgoing.at[to], lambda slot: spread.at[slot], feat_send.at[3], feat_recv.at[3]
-        )
-    )
     gather.near()
     regroups.append(
         Regroup(
@@ -395,7 +350,7 @@
         )
     )
     gather.far()
-    for regroup in regroups[1:]:
+    for regroup in regroups:
         regroup.wait()
     gather.last()
     own.wait()
@@ -488,8 +443,8 @@
 
 
 def mean_kernel(
-    cols_in, counts_in, tiles, source, degrees_in, hidden, cotangent,
-    mean, grads,
+    cols_in, counts_in, tiles, source, degrees_in,
+    mean,
     cols, counts, degrees, held, sums, groups, tile_sems, load_sems,
 ):
     load_all(((cols_in, cols), (counts_in, counts), (degrees_in, degrees)), load_sems)
@@ -508,28 +463,19 @@
     def _(block):
         mean[block] = (sums[block] / degrees[pl.ds(block, 1), :].astype(F32)).astype(BF16)
 
-    wide = 8
-    total = jnp.zeros((2 * hidden.shape[1], cotangent.shape[-1]), F32)
-
-    def add(part, total):
-        blocks = [part * wide + block for block in range(wide)]
-        stack = [jnp.concatenate([hidden[block], mean[block]], axis=0) for block in blocks]
-        nodes = cotangent[pl.ds(part * wide, wide)].reshape(wide * BLK, -1)
-        return total + dot(jnp.concatenate(stack, axis=1), nodes, ((1,), (0,)))
-
-    put_tiles(grads, lax.fori_loop(0, NB // wide, add, total))
-
-
-def put_tiles(out, value):
-    for tile in range(out.shape[0]):
-        out[tile] = value[tile // 2 * 8 : tile // 2 * 8 + 8, tile % 2 * BLK : tile % 2 * BLK + BLK]
+
+def put_tiles(out, kind, first, value):
+    for tile in range(value.shape[0] // 4):
+        out[first + tile, kind] = value[tile // 2 * 8 : tile // 2 * 8 + 8, tile % 2 * BLK : tile % 2 * BLK + BLK]
 
 
 def middle_kernel(
     cols, counts, tiles, all_feats, degrees, back_parts, own_feats, weights1, bias1, weights2, cotangent_in,
-    all_hidden, hidden, own_hidden, all_cotangent, grad_first,
-    held, cotangent, feat_mean, means, slopes, back, own_back, grads, feat_buf, bufs,
-    gather_send, gather_recv, scatter_send, scatter_recv, feat_send, feat_recv, tile_sems, local_sems,
+    all_hidden, hidden, piece,
+    held, cotangent, feat_mean, means, slopes, selves, own_hidden, back, own_back,
+    grads, feat_buf, early, early_buf, part, came, bufs,
+    gather_send, gather_recv, scatter_send, scatter_recv, feat_send, feat_recv, total_send, total_recv,
+    tile_sems, local_sems,
 ):
     place, copies = Place(), Copies()
 
@@ -541,7 +487,7 @@
         tile_copy(step).start()
     load = pltpu.make_async_copy(cotangent_in, cotangent, local_sems.at[0])
     load.start()
-    place.greet(place.beside())
+    place.greet(place.others())
 
     def regroup(number, source_at, target_at):
         return Regroup(copies, place, source_at, target_at, feat_send.at[number], feat_recv.at[number])
@@ -587,6 +533,7 @@
     lax.fori_loop(3, FEATS - 1, send_blocks, jnp.int32(0))
     own_blocks(FEATS - 1)
     means[place.feat] = feat_mean[own_rows(place.feat)]
+    scatter.middle()
     for step in range(FEATS - 1):
         mean_copy(step).wait()
 
@@ -599,67 +546,69 @@
     for block in range(OWN):
         pre = dot(first, stack(block), ((0,), (0,))) + bias
         sigmoid = jax.nn.sigmoid(pre)
-        slopes[block] = (sigmoid * (1.0 + pre * (1.0 - sigmoid))).astype(BF16)
+        slopes[:, block * BLK : (block + 1) * BLK] = (sigmoid * (1.0 + pre * (1.0 - sigmoid))).astype(BF16)
         hidden[:, block] = (pre * sigmoid).astype(BF16).reshape(FEATS, -1, BLK)
     to_hidden = regroup(1, lambda to: hidden.at[to], lambda slot: own_hidden.at[own_rows(slot)])
-    scatter.middle()
+    own_weights = weights2[:, 0].reshape(-1, weights2.shape[-1])
+    load.wait()
+    selves[...] = dot(own_weights, cotangent[...], ((1,), (1,)))
+    all_blocks = jnp.concatenate([hidden[:, block].reshape(-1, BLK) for block in range(OWN)], axis=1)
+    total = dot(all_blocks, cotangent[...], ((1,), (0,)))
+    early[...] = total.reshape(early.shape)
     to_hidden.wait()
+    to_early = regroup(4, lambda to: early.at[to], lambda slot: early_buf.at[slot])
     gather = Gather(copies, place, own_hidden, all_hidden, gather_send, gather_recv)
-    gather.start()
     own = pltpu.make_async_copy(own_hidden, all_hidden.at[place.node], local_sems.at[1])
     own.start()
-    load.wait()
-    to_cotangent = Broadcast(copies, place, cotangent, all_cotangent, feat_send.at[4], feat_recv.at[4])
-    own_cotangent = pltpu.make_async_copy(cotangent, all_cotangent.at[place.feat], local_sems.at[2])
-    own_cotangent.start()
+    scatter.lines_arrived()
+    gather.start()
     scatter.turn()
+    scatter.middle2()
     gather.start_columns()
     gather.rows()
-    scatter.middle2()
-    gather.near()
     scatter.end(back)
     to_back = regroup(2, lambda to: back.at[own_rows(to)], lambda slot: own_back.at[slot])
+    neighbour = weights2[:, 1].reshape(-1, weights2.shape[-1])
+    first_stack = jnp.concatenate([stack(block) for block in range(OWN)], axis=1)
+    to_back.wait()
+    came_back = jnp.concatenate(
+        [own_back[:, block].reshape(-1, BLK) for block in range(OWN)], axis=1
+    )
+    grad = selves[...] + dot(neighbour, came_back, ((1,), (0,)))
+    grad = (grad * slopes[...].astype(F32)).astype(BF16)
+    first_rows, hid_rows = weights1.shape[1] * weights1.shape[2], weights2.shape[2]
+    grads[:, :first_rows] = dot(first_stack, grad, ((1,), (1,))).reshape(FEATS, first_rows, -1)
+    all_blocks = jnp.concatenate([hidden[:, block].reshape(-1, BLK) for block in range(OWN)], axis=1)
+    grads[:, first_rows:] = dot(all_blocks, came_back, ((1,), (1,))).reshape(FEATS, hid_rows, -1)
+    to_total = regroup(3, lambda to: grads.at[to], lambda slot: feat_buf.at[slot])
+    part[...] = jnp.zeros_like(part)
+    to_early.wait()
+    put_tiles(part, 0, 0, sum(early_buf[slot] for slot in range(FEATS)))
+    gather.near()
     gather.far((1, 2))
-    to_back.wait()
-    own_weights = weights2[:, 0].reshape(-1, weights2.shape[-1])
-    total = None
-    for block in range(OWN):
-        nodes = cotangent[block * BLK : (block + 1) * BLK, :]
-        came = jnp.concatenate([own_back[part, block] for part in range(FEATS)], axis=0)
-        grad = dot(own_weights, nodes, ((1,), (1,))) + came.astype(F32)
-        grad = (grad * slopes[block].astype(F32)).astype(BF16)
-        product = dot(stack(block), grad, ((1,), (1,)))
-        total = product if total is None else total + product
-    grads[...] = total.reshape(grads.shape)
-    to_total = regroup(3, lambda to: grads.at[to], lambda slot: feat_buf.at[slot])
+    to_total.wait()
+    summed = sum(feat_buf[slot] for slot in range(FEATS))
+    put_tiles(part, 0, hid_rows // 4, summed[first_rows:])
+    put_tiles(part, 1, 0, summed[:first_rows])
+    exchange = Exchange(copies, place, lambda node: part.at[node], came, total_send, total_recv)
+    came[place.node] = part[place.node]
     gather.far((3,))
-    to_cotangent.forward()
-    to_total.wait()
-    put_tiles(grad_first, sum(feat_buf[slot] for slot in range(FEATS)))
     gather.last()
-    to_cotangent.wait()
-    own_cotangent.wait()
+    exchange.wait()
+    piece[...] = sum(came[slot] for slot in range(SIDE * SIDE))
     own.wait()
     copies.finish()
 
 
-def last_kernel(
-    hidden_mean, grad_first, grad_second,
-    means, summed,
-    part, came, feat_send, feat_recv, total_send, total_recv,
-):
+def last_kernel(hidden_mean, piece, means, summed, feat_send, feat_recv, total_send, total_recv):
     place, copies = Place(), Copies()
     place.greet(place.others())
     to_means = Regroup(
         copies, place, lambda to: hidden_mean.at[own_rows(to)], lambda slot: means.at[slot], feat_send, feat_recv
     )
-    part[:, 1] = jnp.zeros_like(part[:, 1])
-    part[:, 0] = grad_second[...]
-    part[pl.ds(0, grad_first.shape[0]), 1] = grad_first[...]
-    total = Total(copies, place, part, came, summed, total_send, total_recv)
-    total.start()
-    total.turn()
-    total.end()
+    exchange = Exchange(copies, place, lambda node: piece, summed, total_send, total_recv)
+    summed[place.node] = piece[...]
+    exchange.wait()
     to_means.wait()
     copies.finish()
 
@@ -751,7 +700,7 @@
     back_parts = pl.pallas_call(
         back_kernel,
         out_shape=shape(block_total, hid_part, BLK),
-        in_specs=[HBM, HBM, ANY, VMEM],
+        in_specs=[HBM, HBM, HBM, VMEM],
         out_specs=VMEM,
         scratch_shapes=[
             *listed,
@@ -763,7 +712,7 @@
         ],
         compiler_params=limit(28),
         name="aggregate_back",
-    )(in_hbm(slot_cols), in_hbm(tile_counts), groups, spread.reshape(NB, hid_part, BLK))
+    )(in_hbm(slot_cols), in_hbm(tile_counts), in_hbm(groups), spread.reshape(NB, hid_part, BLK))
 
     row = (SIDE, HALF, hid_part, BLK)
     part_row = (SIDE, QUARTER, hid_part, BLK)
@@ -777,27 +726,32 @@
         buf(2, 2, *part_row[1:]),
     )
     first_rows, second_rows = 2 * feat_part, 2 * hid_part
-    all_hidden, hidden, own_hidden, all_cotangent, first_part = pl.pallas_call(
+    pieces = (shard_total, 2, 8, BLK)
+    all_hidden, hidden, piece = pl.pallas_call(
         middle_kernel,
         out_shape=(
             shape(shard_total, NB, hid_part, BLK),
             shape(FEATS, OWN, hid_part, BLK),
-            shape(NB, hid_part, BLK),
-            shape(FEATS, own_nodes, width),
-            shape(first_rows // 8 * 2, 8, BLK, dtype=F32),
+            shape(*pieces[1:], dtype=F32),
         ),
-        in_specs=[SMEM, SMEM, ANY] + [VMEM] * 7 + [HBM],
-        out_specs=(ANY, VMEM, VMEM, ANY, VMEM),
+        in_specs=[SMEM, SMEM, HBM] + [VMEM] * 7 + [HBM],
+        out_specs=(ANY, VMEM, VMEM),
         scratch_shapes=[
             buf(ROW_STAGES, OWN, *tiles.shape[1:]),
             buf(own_nodes, width),
             buf(NB, feat_part, BLK),
             buf(FEATS, OWN, feat_part, BLK),
-            buf(OWN, width, BLK),
+            buf(width, own_nodes),
+            buf(width, own_nodes, dtype=F32),
+            buf(NB, hid_part, BLK),
             buf(NB, hid_part, BLK),
             buf(FEATS, OWN, hid_part, BLK),
-            buf(FEATS, first_rows, width, dtype=F32),
-            buf(FEATS, first_rows, width, dtype=F32),
+            buf(FEATS, first_rows + hid_part, width, dtype=F32),
+            buf(FEATS, first_rows + hid_part, width, dtype=F32),
+            buf(FEATS, hid_part, width, dtype=F32),
+            buf(FEATS, hid_part, width, dtype=F32),
+            buf(*pieces, dtype=F32),
+            buf(*pieces, dtype=F32),
             middle_bufs,
             dma(2, 5, 4),
             dma(2, 5, 4),
@@ -805,15 +759,17 @@
             dma(2, 2, 2, 3),
             dma(5, FEATS - 1),
             dma(5, FEATS - 1),
+            dma(shard_total - 1),
+            dma(shard_total - 1),
             dma(ROW_STAGES),
-            dma(3),
+            dma(2),
         ],
-        compiler_params=limit(32, 2),
+        compiler_params=limit(36, 2),
         name="first_layer",
     )(
         slot_cols,
         tile_counts,
-        tiles,
+        in_hbm(tiles),
         all_feats.reshape(block_total, feat_part, BLK),
         degree_rows,
         back_parts.reshape(SIDE, SIDE, NB, hid_part, BLK),
@@ -824,11 +780,11 @@
         in_hbm(cotangent),
     )
 
-    hidden_mean, second_part = pl.pallas_call(
+    hidden_mean = pl.pallas_call(
         mean_kernel,
-        out_shape=(shape(NB, hid_part, BLK), shape(second_rows // 8 * 2, 8, BLK, dtype=F32)),
-        in_specs=[HBM, HBM, ANY, VMEM, HBM, VMEM, VMEM],
-        out_specs=(VMEM, VMEM),
+        out_shape=shape(NB, hid_part, BLK),
+        in_specs=[HBM, HBM, HBM, VMEM, HBM],
+        out_specs=VMEM,
         scratch_shapes=[
             *listed,
             buf(NB, BLK, dtype=jnp.int32),
@@ -838,35 +794,25 @@
             dma(STAGES),
             dma(3),
         ],
-        compiler_params=limit(24),
+        compiler_params=limit(20),
         name="aggregate_hidden",
     )(
         in_hbm(slot_cols),
         in_hbm(tile_counts),
-        groups,
+        in_hbm(groups),
         all_hidden.reshape(block_total, hid_part, BLK),
         in_hbm(degree_rows),
-        own_hidden,
-        all_cotangent.reshape(NB, BLK, width),
-    )
-
-    pieces = (shard_total, 2, 8, BLK)
+    )
+
     means, summed = pl.pallas_call(
         last_kernel,
         out_shape=(shape(FEATS, OWN, hid_part, BLK), shape(*pieces, dtype=F32)),
-        in_specs=[VMEM] * 3,
+        in_specs=[VMEM] * 2,
         out_specs=(VMEM, VMEM),
-        scratch_shapes=[
-            buf(*pieces, dtype=F32),
-            buf(*pieces, dtype=F32),
-            dma(FEATS - 1),
-            dma(FEATS - 1),
-            dma(2, shard_total - 1),
-            dma(2, shard_total - 1),
-        ],
+        scratch_shapes=[dma(FEATS - 1), dma(FEATS - 1), dma(shard_total - 1), dma(shard_total - 1)],
         compiler_params=limit(8, 3),
         name="regroup_mean",
-    )(hidden_mean, first_part, second_part)
+    )(hidden_mean, piece)
     hidden_out, grad_second, grad_first = pl.pallas_call(
         functools.partial(out_kernel, scale),
         out_shape=(

time: 136 us -> 137 us (level); the launches traced: 136 us -> 135 us
    pallas_call x1, Pallas kernels: 72.4 us -> 77.2 us  [shards(): pl.pallas_call(middle_kernel, out_shape=(shape(shard_total, NB, hid_part,...]
    pallas_call x1, Pallas kernels: 19 us -> 14.4 us  [shards(): pl.pallas_call(last_kernel, out_shape=(shape(FEATS, OWN, hid_part, BLK),...]
where the time goes in v4:
time: 137 us; the launch traced here: 135 us
  Pallas kernels  134 us (98%)
    pallas_call x1, Pallas kernels, shards(): pl.pallas_call(middle_kernel, out_shape=(shape(shard_total, NB, hid_part,...  77.2 us
    pallas_call x1, Pallas kernels, shards(): pl.pallas_call(gather_kernel, out_shape=(shape(shard_total, NB, feat_part...  28.9 us
    pallas_call x1, Pallas kernels, shards(): pl.pallas_call(last_kernel, out_shape=(shape(FEATS, OWN, hid_part, BLK),...  14.4 us
    pallas_call x1, Pallas kernels, shards(): pl.pallas_call(mean_kernel, out_shape=shape(NB, hid_part, BLK), in_specs=...  6.34 us
    pallas_call x1, Pallas kernels, shards(): pl.pallas_call(back_kernel, out_shape=shape(block_total, hid_part, BLK),...  6.09 us

profile of v4, /device:TPU:0, one launch (start us, length us, event | category | flops | bytes accessed | tf_op | source)
XLA Modules:
  0.0 135.0 jit_solution(3355274470824041537)
XLA Ops:
  0.6 28.9 %gather_features.1 = (bf16[16,48,16,128]{3,2,1,0:T(8,128)(2,1)S(1)}, bf16[8,6,16,128]{3,2,1,0:T(8,128)(2,1)S(1)}, bf16[8,2,16,256]{3,2,1,0:T(8,128)(2,1)S(1)}, b...) custom-call(bf16[16,6144]{1,0:T(8,128)(2,1)} %features_in.1, bf16[2,16,256]{2,1,0:T(8,128)(2,1)} %weights1.1, ...), custom_call_target="tpu_custom_call" | custom-call | tf_op jit(solution)/shard_map/gather_features/pallas_call | solution.py:667
  29.6 0.0 copy-start
  29.6 0.0 copy-start.1
  29.6 0.0 copy-start.2
  29.6 0.0 copy-start.3
  29.6 6.1 %aggregate_back.1 = bf16[768,32,128]{2,1,0:T(8,128)(2,1)S(1)} custom-call(s32[16,48]{1,0:T(8,128)} %bitcast.18, s32[48]{0:T(128)} %counts_in.3, bf16[192,4,128,128]{3,2,1,0:T(8,128)(2,1)} %bitcast.23, bf16[48,32,128]{2,1,0:T(8,128)(2,1)S(1)} %bitcast.14), custom_call_target="tpu_custom_call" | custom-call | tf_op jit(solution)/shard_map/aggregate_back/pallas_call | solution.py:700
  35.7 0.0 copy-done
  35.7 0.0 copy-done.1
  35.7 0.0 copy-done.2
  35.7 0.0 copy-done.3
  35.8 77.2 %first_layer.1 = (bf16[16,48,32,128]{3,2,1,0:T(8,128)(2,1)S(1)}, bf16[8,6,32,128]{3,2,1,0:T(8,128)(2,1)S(1)}, f32[2,8,128]{2,1,0:T(8,128)S(1)}) custom-call(s32[16,48]{1,0:T(8,128)S(1)} %bitcast.20, s32[48]{0:T(128)S(1)} %copy-done.2, bf16[48,16,128,128]{3,2,1,0:T(8,128)(2,1)} %tiles.1, bf16[768,16,128]{2,1,0:T(8,128)(2,1)S(1)} %bitcast.13, ...), custom_call_target="tpu_custom_call" | custom-call | tf_op jit(solution)/shard_map/first_layer/pallas_call | solution.py:730
  113.0 0.0 copy-start.4
  113.0 6.3 %aggregate_hidden.1.hidden_mean = bf16[48,32,128]{2,1,0:T(8,128)(2,1)S(1)} custom-call(s32[16,48]{1,0:T(8,128)} %bitcast.19, s32[48]{0:T(128)} %counts_in.3, bf16[192,4,128,128]{3,2,1,0:T(8,128)(2,1)} %bitcast.24, bf16[768,32,128]{2,1,0:T(8,128)(2,1)S(1)} %bitcast.12, s32[48,128]{1,0:T(8,128)} %bitcast.16), custom_call_target="tpu_custom_call" | custom-call | tf_op jit(solution)/shard_map/aggregate_hidden/pallas_call | solution.py:783
  119.4 14.4 %regroup_mean.1 = (bf16[8,6,32,128]{3,2,1,0:T(8,128)(2,1)S(1)}, f32[16,2,8,128]{3,2,1,0:T(8,128)S(1)}) custom-call(bf16[48,32,128]{2,1,0:T(8,128)(2,1)S(1)} %aggregate_hidden.1.hidden_mean, f32[2,8,128]{2,1,0:T(8,128)S(1)} %get-tuple-element.23.piece), custom_call_target="tpu_custom_call" | custom-call | tf_op jit(solution)/shard_map/regroup_mean/pallas_call | solution.py:807
  133.8 0.0 copy-done.4
  133.8 1.2 second_layer.1
Async XLA Ops:
  29.6 6.2 %copy-start = (s32[6144]{0:T(1024)S(1)}, s32[6144]{0:T(1024)}, u32[]{:S(2)}) copy-start(s32[6144]{0:T(1024)} %param.14) | copy-start | bytes 73732
  29.6 6.1 %copy-start.1 = (s32[48,16]{0,1:T(8,128)S(1)}, s32[48,16]{0,1:T(8,128)}, u32[]{:S(2)}) copy-start(s32[48,16]{0,1:T(8,128)} %param.11) | copy-start | bytes 9220
  29.6 6.1 %copy-start.2 = (s32[48]{0:T(128)S(1)}, s32[48]{0:T(128)}, u32[]{:S(2)}) copy-start(s32[48]{0:T(128)} %counts_in.3) | copy-start | bytes 580
  29.6 6.1 %copy-start.3 = (f32[256]{0:T(256)S(1)}, f32[256]{0:T(256)}, u32[]{:S(2)}) copy-start(f32[256]{0:T(256)} %param.16) | copy-start | bytes 3076
  113.0 20.8 %copy-start.4 = (f32[256]{0:T(256)S(1)}, f32[256]{0:T(256)}, u32[]{:S(2)}) copy-start(f32[256]{0:T(256)} %param.18) | copy-start | bytes 3076

commit v5 on v4

--- a/solution.py
+++ b/solution.py
@@ -277,6 +277,64 @@
                 near = self.got2[half, 0, rows].astype(F32) + self.got2[half, 1, rows].astype(F32)
                 total = self._unit(half, 0, quarter)[...].astype(F32) + near
                 out[pl.ds(half * HALF + quarter * QUARTER, QUARTER)] = total.astype(BF16)
+
+
+class Rows:
+    def __init__(self, place, cols, counts, tiles, source, degrees, mean, means, held, send_sems, recv_sems, tile_sems):
+        self.place, self.cols, self.counts, self.tiles, self.source = place, cols, counts, tiles, source
+        self.degrees, self.mean, self.means, self.held = degrees, mean, means, held
+        self.send_sems, self.recv_sems, self.tile_sems = send_sems, recv_sems, tile_sems
+        for step in range(ROW_STAGES - 1):
+            self.fetch(step).start()
+
+    def fetch(self, step):
+        slot = step % ROW_STAGES
+        rows = own_rows(self.place.peer(step + 1))
+        return pltpu.make_async_copy(self.tiles.at[rows], self.held.at[slot], self.tile_sems.at[slot])
+
+    def give(self, step):
+        to = self.place.peer(step + 1)
+        return pltpu.make_async_remote_copy(
+            src_ref=self.mean.at[own_rows(to)],
+            dst_ref=self.means.at[self.place.feat],
+            send_sem=self.send_sems.at[step],
+            recv_sem=self.recv_sems.at[step],
+            device_id={"feat": to},
+            device_id_type=MESH,
+        )
+
+    def work(self, step):
+        self.fetch(step).wait()
+        slots = self.tiles.shape[1]
+        for part in range(OWN):
+            block = self.place.peer(step + 1) * OWN + part
+            parts = []
+            for slot in range(slots):
+                value = self.source[self.cols[slot, block]]
+                parts.append(jnp.where(slot < self.counts[block], value, jnp.zeros_like(value)))
+            wide = jnp.concatenate([self.held[step % ROW_STAGES, part, slot] for slot in range(slots)], axis=1)
+            total = dot(jnp.concatenate(parts, axis=1), wide, ((1,), (1,)))
+            self.mean[block] = (total / self.degrees[pl.ds(block, 1), :].astype(F32)).astype(BF16)
+
+    def run(self, first, last):
+        def body(step, carry):
+            @pl.when(step + ROW_STAGES - 1 < FEATS)
+            def _():
+                self.fetch(step + ROW_STAGES - 1).start()
+
+            self.work(step)
+            self.give(step).start()
+            return carry
+
+        lax.fori_loop(first, last, body, jnp.int32(0))
+
+    def own(self):
+        self.work(FEATS - 1)
+        self.means[self.place.feat] = self.mean[own_rows(self.place.feat)]
+
+    def wait(self):
+        for step in range(FEATS - 1):
+            self.give(step).wait()
 
 
 class Exchange:
@@ -402,15 +460,6 @@
     lax.fori_loop(0, steps, body, jnp.int32(0))
 
 
-def picked(source, cols, entry):
-    block, first, live, wide = entry
-    parts = []
-    for slot in range(GROUP):
-        value = source[cols[first + slot, block]]
-        parts.append(jnp.where(first + slot < live, value, jnp.zeros_like(value)))
-    return dot(jnp.concatenate(parts, axis=1), wide, ((1,), (1,)))
-
-
 def load_all(pairs, sems):
     loads = [pltpu.make_async_copy(pair[0], pair[1], sems.at[number]) for number, pair in enumerate(pairs)]
     for load in loads:
@@ -440,28 +489,6 @@
     def _(part):
         rows = pl.ds(part * 16, 16)
         back[rows] = sums[rows].astype(BF16)
-
-
-def mean_kernel(
-    cols_in, counts_in, tiles, source, degrees_in,
-    mean,
-    cols, counts, degrees, held, sums, groups, tile_sems, load_sems,
-):
-    load_all(((cols_in, cols), (counts_in, counts), (degrees_in, degrees)), load_sems)
-
-    def clear():
-        sums[...] = jnp.zeros_like(sums)
-
-    def work(entries):
-        products = [picked(source, cols, entry) for entry in entries]
-        for entry, product in zip(entries, products):
-            sums[entry[0]] += product
-
-    each_step(counts, groups, tiles, held, tile_sems, clear, work)
-
-    @pl.loop(0, NB)
-    def _(block):
-        mean[block] = (sums[block] / degrees[pl.ds(block, 1), :].astype(F32)).astype(BF16)
 
 
 def put_tiles(out, kind, first, value):
@@ -479,63 +506,26 @@
 ):
     place, copies = Place(), Copies()
 
-    def tile_copy(step):
-        slot = step % ROW_STAGES
-        return pltpu.make_async_copy(tiles.at[own_rows(place.peer(step + 1))], held.at[slot], tile_sems.at[slot])
-
-    for step in range(ROW_STAGES - 1):
-        tile_copy(step).start()
+    rows = Rows(
+        place, cols, counts, tiles, all_feats, degrees, feat_mean, means, held, feat_send.at[0], feat_recv.at[0], tile_sems
+    )
     load = pltpu.make_async_copy(cotangent_in, cotangent, local_sems.at[0])
     load.start()
     place.greet(place.others())
 
     def regroup(number, source_at, target_at):
         return Regroup(copies, place, source_at, target_at, feat_send.at[number], feat_recv.at[number])
-
-    def mean_copy(step):
-        to = place.peer(step + 1)
-        return pltpu.make_async_remote_copy(
-            src_ref=feat_mean.at[own_rows(to)],
-            dst_ref=means.at[place.feat],
-            send_sem=feat_send.at[0, step],
-            recv_sem=feat_recv.at[0, step],
-            device_id={"feat": to},
-            device_id_type=MESH,
-        )
-
-    def own_blocks(step):
-        tile_copy(step).wait()
-        for part in range(OWN):
-            block = place.peer(step + 1) * OWN + part
-            parts = []
-            for slot in range(tiles.shape[1]):
-                value = all_feats[cols[slot, block]]
-                parts.append(jnp.where(slot < counts[block], value, jnp.zeros_like(value)))
-            wide = jnp.concatenate([held[step % ROW_STAGES, part, slot] for slot in range(tiles.shape[1])], axis=1)
-            total = dot(jnp.concatenate(parts, axis=1), wide, ((1,), (1,)))
-            feat_mean[block] = (total / degrees[pl.ds(block, 1), :].astype(F32)).astype(BF16)
-
-    def send_blocks(step, carry):
-        @pl.when(step + ROW_STAGES - 1 < FEATS)
-        def _():
-            tile_copy(step + ROW_STAGES - 1).start()
-
-        own_blocks(step)
-        mean_copy(step).start()
-        return carry
 
     scatter = Scatter(copies, place, back_parts, bufs, scatter_send, scatter_recv)
     scatter.start()
     first = weights1[...].reshape(-1, weights1.shape[-1])
     bias = jnp.transpose(jnp.broadcast_to(bias1[...], (BLK, bias1.shape[1])))
-    lax.fori_loop(0, 3, send_blocks, jnp.int32(0))
+    rows.run(0, 3)
     scatter.direct()
-    lax.fori_loop(3, FEATS - 1, send_blocks, jnp.int32(0))
-    own_blocks(FEATS - 1)
-    means[place.feat] = feat_mean[own_rows(place.feat)]
+    rows.run(3, FEATS - 1)
+    rows.own()
     scatter.middle()
-    for step in range(FEATS - 1):
-        mean_copy(step).wait()
+    rows.wait()
 
     def stack(block):
         parts = []
@@ -600,16 +590,22 @@
     copies.finish()
 
 
-def last_kernel(hidden_mean, piece, means, summed, feat_send, feat_recv, total_send, total_recv):
+def last_kernel(
+    cols, counts, tiles, all_hidden, degrees, piece,
+    means, summed,
+    held, hidden_mean, feat_send, feat_recv, total_send, total_recv, tile_sems,
+):
     place, copies = Place(), Copies()
+    rows = Rows(
+        place, cols, counts, tiles, all_hidden, degrees, hidden_mean, means, held, feat_send, feat_recv, tile_sems
+    )
     place.greet(place.others())
-    to_means = Regroup(
-        copies, place, lambda to: hidden_mean.at[own_rows(to)], lambda slot: means.at[slot], feat_send, feat_recv
-    )
     exchange = Exchange(copies, place, lambda node: piece, summed, total_send, total_recv)
     summed[place.node] = piece[...]
+    rows.run(0, FEATS - 1)
+    rows.own()
+    rows.wait()
     exchange.wait()
-    to_means.wait()
     copies.finish()
 
 
@@ -780,39 +776,30 @@
         in_hbm(cotangent),
     )
 
-    hidden_mean = pl.pallas_call(
-        mean_kernel,
-        out_shape=shape(NB, hid_part, BLK),
-        in_specs=[HBM, HBM, HBM, VMEM, HBM],
-        out_specs=VMEM,
-        scratch_shapes=[
-            *listed,
-            buf(NB, BLK, dtype=jnp.int32),
-            held,
-            buf(NB, hid_part, BLK, dtype=F32),
-            planned,
-            dma(STAGES),
-            dma(3),
-        ],
-        compiler_params=limit(20),
-        name="aggregate_hidden",
-    )(
-        in_hbm(slot_cols),
-        in_hbm(tile_counts),
-        in_hbm(groups),
-        all_hidden.reshape(block_total, hid_part, BLK),
-        in_hbm(degree_rows),
-    )
-
     means, summed = pl.pallas_call(
         last_kernel,
         out_shape=(shape(FEATS, OWN, hid_part, BLK), shape(*pieces, dtype=F32)),
-        in_specs=[VMEM] * 2,
+        in_specs=[SMEM, SMEM, HBM, VMEM, VMEM, VMEM],
         out_specs=(VMEM, VMEM),
-        scratch_shapes=[dma(FEATS - 1), dma(FEATS - 1), dma(shard_total - 1), dma(shard_total - 1)],
-        compiler_params=limit(8, 3),
-        name="regroup_mean",
-    )(hidden_mean, piece)
+        scratch_shapes=[
+            buf(ROW_STAGES, OWN, *tiles.shape[1:]),
+            buf(NB, hid_part, BLK),
+            dma(FEATS - 1),
+            dma(FEATS - 1),
+            dma(shard_total - 1),
+            dma(shard_total - 1),
+            dma(ROW_STAGES),
+        ],
+        compiler_params=limit(28, 3),
+        name="aggregate_hidden",
+    )(
+        slot_cols,
+        tile_counts,
+        in_hbm(tiles),
+        all_hidden.reshape(block_total, hid_part, BLK),
+        degree_rows,
+        piece,
+    )
     hidden_out, grad_second, grad_first = pl.pallas_call(
         functools.partial(out_kernel, scale),
         out_shape=(

time: 137 us -> 131 us (0.956)
  Pallas kernels: 134 us -> 128 us
    pallas_call x1 -> x0, Pallas kernels: 6.34 us -> none  [shards(): pl.pallas_call(mean_kernel, out_shape=shape(NB, hid_part, BLK), in_specs=...]
where the time goes in v5:
time: 131 us; the launch traced here: 129 us
  Pallas kernels  128 us (98%)
    pallas_call x1, Pallas kernels, shards(): pl.pallas_call(middle_kernel, out_shape=(shape(shard_total, NB, hid_part,...  77.7 us
    pallas_call x1, Pallas kernels, shards(): pl.pallas_call(gather_kernel, out_shape=(shape(shard_total, NB, feat_part...  28.9 us
    pallas_call x1, Pallas kernels, shards(): pl.pallas_call(last_kernel, out_shape=(shape(FEATS, OWN, hid_part, BLK),...  14.2 us
    pallas_call x1, Pallas kernels, shards(): pl.pallas_call(back_kernel, out_shape=shape(block_total, hid_part, BLK),...  6.09 us

profile of v5, /device:TPU:0, one launch (start us, length us, event | category | flops | bytes accessed | tf_op | source)
XLA Modules:
  0.0 128.9 jit_solution(15989184253162703531)
XLA Ops:
  0.6 28.9 %gather_features.1 = (bf16[16,48,16,128]{3,2,1,0:T(8,128)(2,1)S(1)}, bf16[8,6,16,128]{3,2,1,0:T(8,128)(2,1)S(1)}, bf16[8,2,16,256]{3,2,1,0:T(8,128)(2,1)S(1)}, b...) custom-call(bf16[16,6144]{1,0:T(8,128)(2,1)} %features_in.1, bf16[2,16,256]{2,1,0:T(8,128)(2,1)} %weights1.1, ...), custom_call_target="tpu_custom_call" | custom-call | tf_op jit(solution)/shard_map/gather_features/pallas_call | solution.py:663
  29.6 0.0 copy-start
  29.6 0.0 copy-start.1
  29.6 0.0 copy-start.2
  29.6 0.0 copy-start.3
  29.6 6.1 %aggregate_back.1 = bf16[768,32,128]{2,1,0:T(8,128)(2,1)S(1)} custom-call(s32[16,48]{1,0:T(8,128)} %bitcast.18, s32[48]{0:T(128)} %counts.3, bf16[192,4,128,128]{3,2,1,0:T(8,128)(2,1)} %bitcast.23, bf16[48,32,128]{2,1,0:T(8,128)(2,1)S(1)} %bitcast.14), custom_call_target="tpu_custom_call" | custom-call | tf_op jit(solution)/shard_map/aggregate_back/pallas_call | solution.py:696
  35.7 0.0 copy-done
  35.7 0.0 copy-done.1
  35.7 0.0 copy-done.2
  35.7 0.0 copy-done.3
  35.8 77.7 %first_layer.1 = (bf16[16,48,32,128]{3,2,1,0:T(8,128)(2,1)S(1)}, bf16[8,6,32,128]{3,2,1,0:T(8,128)(2,1)S(1)}, f32[2,8,128]{2,1,0:T(8,128)S(1)}) custom-call(s32[16,48]{1,0:T(8,128)S(1)} %bitcast.19, s32[48]{0:T(128)S(1)} %copy-done.2, bf16[48,16,128,128]{3,2,1,0:T(8,128)(2,1)} %tiles.3, bf16[768,16,128]{2,1,0:T(8,128)(2,1)S(1)} %bitcast.13, ...), custom_call_target="tpu_custom_call" | custom-call | tf_op jit(solution)/shard_map/first_layer/pallas_call | solution.py:726
  113.5 0.0 copy-start.4
  113.5 14.2 %aggregate_hidden.1 = (bf16[8,6,32,128]{3,2,1,0:T(8,128)(2,1)S(1)}, f32[16,2,8,128]{3,2,1,0:T(8,128)S(1)}) custom-call(s32[16,48]{1,0:T(8,128)S(1)} %bitcast.20, s32[48]{0:T(128)S(1)} %copy-done.2, bf16[48,16,128,128]{3,2,1,0:T(8,128)(2,1)} %tiles.3, bf16[768,32,128]{2,1,0:T(8,128)(2,1)S(1)} %bitcast.12, s32[48,128]{1,0:T(8,128)S(1)} %bitcast.17, ...), custom_call_target="tpu_custom_call" | custom-call | tf_op jit(solution)/shard_map/aggregate_hidden/pallas_call | solution.py:779
  127.7 0.0 copy-done.4
  127.7 1.2 second_layer.1
Async XLA Ops:
  29.6 6.2 %copy-start = (s32[6144]{0:T(1024)S(1)}, s32[6144]{0:T(1024)}, u32[]{:S(2)}) copy-start(s32[6144]{0:T(1024)} %param.14) | copy-start | bytes 73732
  29.6 6.1 %copy-start.1 = (s32[48,16]{0,1:T(8,128)S(1)}, s32[48,16]{0,1:T(8,128)}, u32[]{:S(2)}) copy-start(s32[48,16]{0,1:T(8,128)} %param.11) | copy-start | bytes 9220
  29.6 6.1 %copy-start.2 = (s32[48]{0:T(128)S(1)}, s32[48]{0:T(128)}, u32[]{:S(2)}) copy-start(s32[48]{0:T(128)} %counts.3) | copy-start | bytes 580
  29.6 6.1 %copy-start.3 = (f32[256]{0:T(256)S(1)}, f32[256]{0:T(256)}, u32[]{:S(2)}) copy-start(f32[256]{0:T(256)} %param.16) | copy-start | bytes 3076
  113.5 14.3 %copy-start.4 = (f32[256]{0:T(256)S(1)}, f32[256]{0:T(256)}, u32[]{:S(2)}) copy-start(f32[256]{0:T(256)} %param.18) | copy-start | bytes 3076

commit v6 on v5

--- a/solution.py
+++ b/solution.py
@@ -61,7 +61,10 @@
         others += [{"node": node} for node in nodes]
         for other in others:
             pl.semaphore_signal(barrier, inc=1, device_id=other, device_id_type=MESH)
-        pl.semaphore_wait(barrier, len(others))
+        self.greeted = len(others)
+
+    def meet(self):
+        pl.semaphore_wait(pltpu.get_barrier_semaphore(), self.greeted)
 
 
 class Copies:
@@ -316,6 +319,10 @@
             total = dot(jnp.concatenate(parts, axis=1), wide, ((1,), (1,)))
             self.mean[block] = (total / self.degrees[pl.ds(block, 1), :].astype(F32)).astype(BF16)
 
+    def first(self):
+        self.fetch(ROW_STAGES - 1).start()
+        self.work(0)
+
     def run(self, first, last):
         def body(step, carry):
             @pl.when(step + ROW_STAGES - 1 < FEATS)
@@ -377,6 +384,7 @@
     loads[0].wait()
     for block in range(NB):
         blocks[block] = features[:, block * BLK : (block + 1) * BLK]
+    place.meet()
     gather = Gather(copies, place, blocks, all_feats, gather_send, gather_recv)
     gather.start()
     gather.start_columns()
@@ -512,6 +520,7 @@
     load = pltpu.make_async_copy(cotangent_in, cotangent, local_sems.at[0])
     load.start()
     place.greet(place.others())
+    place.meet()
 
     def regroup(number, source_at, target_at):
         return Regroup(copies, place, source_at, target_at, feat_send.at[number], feat_recv.at[number])
@@ -600,9 +609,12 @@
         place, cols, counts, tiles, all_hidden, degrees, hidden_mean, means, held, feat_send, feat_recv, tile_sems
     )
     place.greet(place.others())
+    rows.first()
+    place.meet()
+    rows.give(0).start()
     exchange = Exchange(copies, place, lambda node: piece, summed, total_send, total_recv)
     summed[place.node] = piece[...]
-    rows.run(0, FEATS - 1)
+    rows.run(1, FEATS - 1)
     rows.own()
     rows.wait()
     exchange.wait()

time: 131 us -> 131 us (level)
  no operation moved by 1% of the time
where the time goes in v6:
time: 131 us; the launch traced here: 129 us
  Pallas kernels  128 us (98%)
    pallas_call x1, Pallas kernels, shards(): pl.pallas_call(middle_kernel, out_shape=(shape(shard_total, NB, hid_part,...  78.6 us
    pallas_call x1, Pallas kernels, shards(): pl.pallas_call(gather_kernel, out_shape=(shape(shard_total, NB, feat_part...  28.9 us
    pallas_call x1, Pallas kernels, shards(): pl.pallas_call(last_kernel, out_shape=(shape(FEATS, OWN, hid_part, BLK),...  13.4 us
    pallas_call x1, Pallas kernels, shards(): pl.pallas_call(back_kernel, out_shape=shape(block_total, hid_part, BLK),...  6.09 us

profile of v6, /device:TPU:0, one launch (start us, length us, event | category | flops | bytes accessed | tf_op | source)
XLA Modules:
  0.0 129.0 jit_solution(17715316733531564074)
XLA Ops:
  0.6 28.9 %gather_features.1 = (bf16[16,48,16,128]{3,2,1,0:T(8,128)(2,1)S(1)}, bf16[8,6,16,128]{3,2,1,0:T(8,128)(2,1)S(1)}, bf16[8,2,16,256]{3,2,1,0:T(8,128)(2,1)S(1)}, b...) custom-call(bf16[16,6144]{1,0:T(8,128)(2,1)} %features_in.1, bf16[2,16,256]{2,1,0:T(8,128)(2,1)} %weights1.1, ...), custom_call_target="tpu_custom_call" | custom-call | tf_op jit(solution)/shard_map/gather_features/pallas_call | solution.py:675
  29.5 0.0 copy-start
  29.5 0.0 copy-start.1
  29.5 0.0 copy-start.2
  29.6 0.0 copy-start.3
  29.6 6.1 %aggregate_back.1 = bf16[768,32,128]{2,1,0:T(8,128)(2,1)S(1)} custom-call(s32[16,48]{1,0:T(8,128)} %bitcast.18, s32[48]{0:T(128)} %counts.3, bf16[192,4,128,128]{3,2,1,0:T(8,128)(2,1)} %bitcast.23, bf16[48,32,128]{2,1,0:T(8,128)(2,1)S(1)} %bitcast.14), custom_call_target="tpu_custom_call" | custom-call | tf_op jit(solution)/shard_map/aggregate_back/pallas_call | solution.py:708
  35.7 0.0 copy-done
  35.7 0.0 copy-done.1
  35.7 0.0 copy-done.2
  35.7 0.0 copy-done.3
  35.7 78.6 %first_layer.1 = (bf16[16,48,32,128]{3,2,1,0:T(8,128)(2,1)S(1)}, bf16[8,6,32,128]{3,2,1,0:T(8,128)(2,1)S(1)}, f32[2,8,128]{2,1,0:T(8,128)S(1)}) custom-call(s32[16,48]{1,0:T(8,128)S(1)} %bitcast.19, s32[48]{0:T(128)S(1)} %copy-done.2, bf16[48,16,128,128]{3,2,1,0:T(8,128)(2,1)} %tiles.3, bf16[768,16,128]{2,1,0:T(8,128)(2,1)S(1)} %bitcast.13, ...), custom_call_target="tpu_custom_call" | custom-call | tf_op jit(solution)/shard_map/first_layer/pallas_call | solution.py:738
  114.4 0.0 copy-start.4
  114.4 13.4 %aggregate_hidden.1 = (bf16[8,6,32,128]{3,2,1,0:T(8,128)(2,1)S(1)}, f32[16,2,8,128]{3,2,1,0:T(8,128)S(1)}) custom-call(s32[16,48]{1,0:T(8,128)S(1)} %bitcast.20, s32[48]{0:T(128)S(1)} %copy-done.2, bf16[48,16,128,128]{3,2,1,0:T(8,128)(2,1)} %tiles.3, bf16[768,32,128]{2,1,0:T(8,128)(2,1)S(1)} %bitcast.12, s32[48,128]{1,0:T(8,128)S(1)} %bitcast.17, ...), custom_call_target="tpu_custom_call" | custom-call | tf_op jit(solution)/shard_map/aggregate_hidden/pallas_call | solution.py:791
  127.8 0.0 copy-done.4
  127.8 1.2 second_layer.1
Async XLA Ops:
  29.5 6.1 %copy-start = (s32[6144]{0:T(1024)S(1)}, s32[6144]{0:T(1024)}, u32[]{:S(2)}) copy-start(s32[6144]{0:T(1024)} %param.14) | copy-start | bytes 73732
  29.5 6.1 %copy-start.1 = (s32[48,16]{0,1:T(8,128)S(1)}, s32[48,16]{0,1:T(8,128)}, u32[]{:S(2)}) copy-start(s32[48,16]{0,1:T(8,128)} %param.11) | copy-start | bytes 9220
  29.5 6.1 %copy-start.2 = (s32[48]{0:T(128)S(1)}, s32[48]{0:T(128)}, u32[]{:S(2)}) copy-start(s32[48]{0:T(128)} %counts.3) | copy-start | bytes 580
  29.6 6.1 %copy-start.3 = (f32[256]{0:T(256)S(1)}, f32[256]{0:T(256)}, u32[]{:S(2)}) copy-start(f32[256]{0:T(256)} %param.16) | copy-start | bytes 3076
  114.4 13.4 %copy-start.4 = (f32[256]{0:T(256)S(1)}, f32[256]{0:T(256)}, u32[]{:S(2)}) copy-start(f32[256]{0:T(256)} %param.18) | copy-start | bytes 3076
